TPU v7x, 32 devices: a whole 2x2x4 slice. The times are simulated.
32 devices in a mesh: dp: 8 (over z, y), chan: 4 (over x, core).
Axes of the slice: x: 2, y: 2, z: 4, core: 2. Of those that a mesh axis runs over, the one named last changes fastest.
Arguments:
- images: bfloat16 [64, 32, 32, 512], P('dp', None, None, 'chan'), may hold values from -6 to 6
- cotangent: bfloat16 [64, 16, 16, 1024], P('dp', None, None, 'chan'), may hold values from -6 to 6
- groups: int32 [64], P('dp'), may hold values from 0 to 2
- first_reduce: bfloat16 [512, 256], P(None, 'chan'), may hold values from -0.25 to 0.25
- first_reducegain: float32 [256], P('chan'), may hold values from 0.5 to 1.5
- first_reducebias: float32 [256], P('chan'), may hold values from -1.5 to 1.5
- first_split: bfloat16 [3, 3, 128, 2, 256], P(None, None, None, None, 'chan'), may hold values from -0.1875 to 0.1875
- first_splitgain: float32 [2, 256], P(None, 'chan'), may hold values from 0.5 to 1.5
- first_splitbias: float32 [2, 256], P(None, 'chan'), may hold values from -1.5 to 1.5
- first_squeeze: bfloat16 [256, 128], P('chan'), may hold values from -0.375 to 0.375
- first_squeezegain: float32 [128], replicated, may hold values from 0.5 to 1.5
- first_squeezebias: float32 [128], replicated, may hold values from -1.5 to 1.5
- first_excite: bfloat16 [128, 2, 256], P(None, None, 'chan'), may hold values from -0.5 to 0.5
- first_excitebias: float32 [2, 256], P(None, 'chan'), may hold values from -2 to 2
- first_expand: bfloat16 [256, 1024], P(None, 'chan'), may hold values from -0.375 to 0.375
- first_expandgain: float32 [1024], P('chan'), may hold values from 0.5 to 1.5
- first_expandbias: float32 [1024], P('chan'), may hold values from -1.5 to 1.5
- first_shortcut: bfloat16 [512, 1024], P(None, 'chan'), may hold values from -0.25 to 0.25
- first_shortgain: float32 [1024], P('chan'), may hold values from 0.5 to 1.5
- first_shortbias: float32 [1024], P('chan'), may hold values from -1.5 to 1.5
- second_reduce: bfloat16 [1024, 256], P(None, 'chan'), may hold values from -0.1875 to 0.1875
- second_reducegain: float32 [256], P('chan'), may hold values from 0.5 to 1.5
- second_reducebias: float32 [256], P('chan'), may hold values from -1.5 to 1.5
- second_split: bfloat16 [3, 3, 128, 2, 256], P(None, None, None, None, 'chan'), may hold values from -0.1875 to 0.1875
- second_splitgain: float32 [2, 256], P(None, 'chan'), may hold values from 0.5 to 1.5
- second_splitbias: float32 [2, 256], P(None, 'chan'), may hold values from -1.5 to 1.5
- second_squeeze: bfloat16 [256, 128], P('chan'), may hold values from -0.375 to 0.375
- second_squeezegain: float32 [128], replicated, may hold values from 0.5 to 1.5
- second_squeezebias: float32 [128], replicated, may hold values from -1.5 to 1.5
- second_excite: bfloat16 [128, 2, 256], P(None, None, 'chan'), may hold values from -0.5 to 0.5
- second_excitebias: float32 [2, 256], P(None, 'chan'), may hold values from -2 to 2
- second_expand: bfloat16 [256, 1024], P(None, 'chan'), may hold values from -0.375 to 0.375
- second_expandgain: float32 [1024], P('chan'), may hold values from 0.5 to 1.5
- second_expandbias: float32 [1024], P('chan'), may hold values from -1.5 to 1.5
Outputs:
- out_image: float32 [64, 16, 16, 1024], P('dp', None, None, 'chan')
- grad_images: float32 [64, 32, 32, 512], P('dp', None, None, 'chan')
- grad_first_reduce: float32 [512, 256], P(None, 'chan')
- grad_first_reducegain: float32 [256], P('chan')
- grad_first_reducebias: float32 [256], P('chan')
- grad_first_split: float32 [3, 3, 128, 2, 256], P(None, None, None, None, 'chan')
- grad_first_splitgain: float32 [2, 256], P(None, 'chan')
- grad_first_splitbias: float32 [2, 256], P(None, 'chan')
- grad_first_squeeze: float32 [256, 128], P('chan')
- grad_first_squeezegain: float32 [128], replicated
- grad_first_squeezebias: float32 [128], replicated
- grad_first_excite: float32 [128, 2, 256], P(None, None, 'chan')
- grad_first_excitebias: float32 [2, 256], P(None, 'chan')
- grad_first_expand: float32 [256, 1024], P(None, 'chan')
- grad_first_expandgain: float32 [1024], P('chan')
- grad_first_expandbias: float32 [1024], P('chan')
- grad_first_shortcut: float32 [512, 1024], P(None, 'chan')
- grad_first_shortgain: float32 [1024], P('chan')
- grad_first_shortbias: float32 [1024], P('chan')
- grad_second_reduce: float32 [1024, 256], P(None, 'chan')
- grad_second_reducegain: float32 [256], P('chan')
- grad_second_reducebias: float32 [256], P('chan')
- grad_second_split: float32 [3, 3, 128, 2, 256], P(None, None, None, None, 'chan')
- grad_second_splitgain: float32 [2, 256], P(None, 'chan')
- grad_second_splitbias: float32 [2, 256], P(None, 'chan')
- grad_second_squeeze: float32 [256, 128], P('chan')
- grad_second_squeezegain: float32 [128], replicated
- grad_second_squeezebias: float32 [128], replicated
- grad_second_excite: float32 [128, 2, 256], P(None, None, 'chan')
- grad_second_excitebias: float32 [2, 256], P(None, 'chan')
- grad_second_expand: float32 [256, 1024], P(None, 'chan')
- grad_second_expandgain: float32 [1024], P('chan')
- grad_second_expandbias: float32 [1024], P('chan')
Inputs may be any that keep to these rules, and one draw needn't show every extreme that they name: `groups`: an image of group g holds real pixels in the top-left (16 - 4 + 2 g) squared pixels of its output tile and twice that side of its input tile; all other pixels are padding.
All inputs are finite; a program needn't handle non-finite values.
Results may differ from a plain program's by a relative error of at most 0.033.
Values may be sent and summed in bfloat16 or wider, within the bound.
A program may use at most 256 MiB of HBM per device.

v0:
```python
import functools
from types import SimpleNamespace

import jax
import jax.numpy as jnp
from jax import lax
from jax.experimental import pallas as pl
from jax.experimental.pallas import tpu as pltpu
from jax.sharding import PartitionSpec as P

EPSILON = 1e-05
F32, BF16 = jnp.float32, jnp.bfloat16
HIGHEST = lax.Precision.HIGHEST
MESH = pl.DeviceIdType.MESH
LANES = 128
TAPS = 9
DP, CHAN = "dp", "chan"
REDUCE, SPLIT, SQUEEZE, EXCITE, EXPAND, SHORTCUT = range(6)
MATRIX, MID_VECTOR, PAIR_VECTOR, ATT_VECTOR, OUT_VECTOR = range(5)
SYNC_ROWS = (24, 8, 8, 16, 8, 8, 8, 16, 16, 8, 8, 8, 24, 8, 8, 8)

NT = (((1,), (1,)), ((), ()))
NN = (((1,), (0,)), ((), ()))
TN = (((0,), (0,)), ((), ()))


def dot(a, b, dims=NN):
    return lax.dot_general(a, b, dims, preferred_element_type=F32)


def dot_exact(a, b, dims=NN):
    return lax.dot_general(
        a.astype(F32), b.astype(F32), dims, precision=HIGHEST, preferred_element_type=F32
    )


def sigmoid(v):
    return 0.5 * jnp.tanh(0.5 * v) + 0.5


def silu(v):
    return v * sigmoid(v)


def silu_slope(v):
    q = sigmoid(v)
    return q * (1.0 + v * (1.0 - q))


def tiled(v, width):
    return jnp.concatenate([v] * (width // LANES), axis=1) if width > LANES else v


def sum8(v):
    return jnp.sum(v.reshape(v.shape[0] // 8, 8, v.shape[1]), axis=0)


def fold(v):
    return jnp.sum(v, axis=0, keepdims=True)


def span(start, size):
    if isinstance(start, int):
        return pl.ds(start, size)
    return pl.ds(pl.multiple_of(start, size), size)


class Sizes:
    def __init__(self, mesh, images, reduce_w, expand_w, squeeze_w):
        self.nd, self.nc = mesh.shape[DP], mesh.shape[CHAN]
        self.b = images.shape[0] // self.nc
        self.si = images.shape[1]
        self.so = self.si // 2
        self.cis = images.shape[3]
        self.ci = self.cis * self.nc
        self.mids = reduce_w.shape[1]
        self.mid = self.mids * self.nc
        self.cos = expand_w.shape[1]
        self.co = self.cos * self.nc
        self.att = squeeze_w.shape[1]
        self.po = self.so * self.so
        self.pi = self.si * self.si
        self.no = self.b * self.po
        self.ni = self.b * self.pi
        self.grp = self.mid // 2
        self.kk = TAPS * self.grp
        cin = {1: self.ci, 2: self.co}
        self.piece_rows = {
            (k, name): rows
            for k in (1, 2)
            for name, rows in (
                (REDUCE, cin[k] // LANES * self.mids),
                (SPLIT, 2 * TAPS * self.mids),
                (SQUEEZE, self.mids),
                (EXCITE, 2 * self.mids),
                (EXPAND, self.cos // LANES * self.mid),
                (SHORTCUT, self.cos // LANES * self.ci),
            )
        }
        self.lay, self.rows = {}, {}
        for group, members in GROUPS.items():
            at = 0
            for key in members:
                self.lay[key] = (group, at)
                at += self.piece_rows[key]
            self.rows[group] = -(-at // (16 * self.nd)) * 16 * self.nd


GROUPS = {
    0: ((2, EXPAND), (2, EXCITE), (2, SQUEEZE), (2, SPLIT), (2, REDUCE)),
    1: ((1, EXPAND), (1, EXCITE), (1, SHORTCUT)),
    2: ((1, SPLIT), (1, SQUEEZE)),
    3: ((1, REDUCE),),
}
VEC_ROWS = {
    1: SimpleNamespace(rg=0, rb=1, sg=2, sb=4, xb=6, eg=8, eb=10, hg=12, hb=14, qg=16, qb=17),
    2: SimpleNamespace(rg=18, rb=19, sg=20, sb=22, xb=24, eg=26, eb=28, qg=30, qb=31),
}
NVEC = 32
STO_ROWS = {
    2: SimpleNamespace(eb=0, eg=8, qb=16, qg=17, sb=18, sg=22, rb=26, rg=28, xb=30),
    1: SimpleNamespace(eb=34, eg=42, qb=50, qg=51, sb=52, sg=56, rb=60, rg=62, xb=64, hg=68),
}
NSTO = 80
QUARTERS = 4


def space(tree):
    if not isinstance(tree, dict):
        return tree
    inner = {k: space(v) for k, v in tree.items()}
    return SimpleNamespace(**inner) if all(isinstance(k, str) for k in inner) else inner


def scratch_tree(z):
    def f32(*shape):
        return pltpu.VMEM(shape, F32)

    def bf16(*shape):
        return pltpu.VMEM(shape, BF16)

    def sem(*shape):
        return pltpu.SemaphoreType.DMA(shape)

    ns = z.nd * z.nc // 2
    return dict(
        x=bf16(z.ni, z.ci),
        cot=bf16(z.no, z.co),
        wsh=bf16(z.ci, z.co),
        vv=f32(z.nc, NVEC, LANES),
        mo=f32(z.no, LANES),
        mi=bf16(z.ni, LANES),
        red1=f32(z.mid // LANES, z.b * z.so, 2, z.si, LANES),
        u1=f32(z.mid // LANES, z.b * z.so, 2, z.si, LANES),
        pool=bf16(z.no, z.ci),
        short=f32(z.no, z.co),
        h=bf16(z.no, z.co),
        red2=f32(z.no, z.mid),
        u2=f32(z.no, z.mid),
        g=f32(z.no, z.co),
        eg=bf16(z.no, z.co),
        shg=bf16(z.no, z.co),
        mg=f32(z.no, z.mid),
        su=f32(z.no, 2 * z.mid),
        sgb=bf16(z.no, 2 * z.mid),
        sgt=bf16(2 * z.mid, z.no),
        mixt=bf16(z.mid, z.no),
        dcol=f32(z.po + 2 * z.so, z.kk),
        rg1=bf16(z.ni, z.mid),
        rgt=bf16(z.mid, z.ni),
        pg=bf16(z.no, z.ci),
        ags=f32(8, 2 * z.mid),
        mgr=f32(8, z.mid),
        blk={
            k: dict(
                wrt=bf16(z.mid, z.ci if k == 1 else z.co),
                wst=bf16(TAPS, 2, z.mid, z.grp),
                sq=bf16(z.mid, z.att),
                ext=bf16(2, z.mid, z.att),
                we=bf16(z.mid, z.co),
                im=bf16(2, z.no + 2 * z.so, z.kk),
                sp=f32(z.no, 2 * z.mid),
                sa=f32(z.no, 2 * z.mid),
                mix=bf16(z.no, z.mid),
                exp=f32(z.no, z.co),
                att=f32(8, 2 * z.mid),
                pm=f32(8, z.mid),
            )
            for k in (1, 2)
        },
        group={
            n: dict(
                pk=bf16(z.nc // 2, 2, rows, LANES),
                r1=bf16(z.nc // 2, rows, LANES),
                r2=bf16(rows, LANES),
                r3=bf16(z.nd, rows // z.nd, LANES),
                q1=sem(2),
                q2=sem(2),
                q3s=sem(z.nd),
                q3r=sem(z.nd),
                q4s=sem(z.nd),
                q4r=sem(z.nd),
            )
            for n, rows in z.rows.items()
        },
        sync={
            k: dict(sa=f32(rows, LANES), sb=f32(rows, LANES), st=f32(rows, LANES))
            for k, rows in enumerate(SYNC_ROWS)
        },
        slots={p: f32(ns, max(SYNC_ROWS), LANES) for p in range(2)},
        gather_send=sem(13, z.nc),
        gather_recv=sem(13, z.nc),
        image_send=sem(QUARTERS, z.nc),
        image_recv=sem(QUARTERS, z.nc),
        out_send=sem(1 + QUARTERS, z.nc),
        out_got=sem(1 + QUARTERS, z.nc),
        s0s=sem(1),
        s0r=sem(2),
        s1s=sem(ns),
        s1r=sem(2, ns),
    )


def mega_kernel(z, tree, *refs):
    given, made, r = (space(t) for t in jax.tree.unflatten(tree, refs))
    nc, nd = z.nc, z.nd
    b, so, si, po, pi_, no, ni = z.b, z.so, z.si, z.po, z.pi, z.no, z.ni
    mid, co, ci, att, grp, kk = z.mid, z.co, z.ci, z.att, z.grp, z.kk
    d, c = lax.axis_index(DP), lax.axis_index(CHAN)
    ns = nd * nc // 2
    me = d * (nc // 2) + lax.div(c, 2)
    odd = lax.rem(c, 2)

    def chan_at(i):
        return lax.rem(c + i, nc)

    def place(s):
        return (lax.div(s, nc // 2), lax.rem(s, nc // 2) * 2 + odd)

    partner = (d, c + 1 - 2 * odd)

    barrier = pltpu.get_barrier_semaphore()
    for i in range(1, nc):
        pl.semaphore_signal(barrier, inc=1, device_id=(d, chan_at(i)), device_id_type=MESH)

    def greet(j, _):
        pl.semaphore_signal(
            barrier, inc=1, device_id=place(lax.rem(me + j, ns)), device_id_type=MESH
        )
        return 0

    lax.fori_loop(1, ns, greet, 0)
    pl.semaphore_wait(barrier, nc - 1 + ns - 1)

    class Exchange:
        def __init__(self, src, dst, send, recv):
            self.src, self.dst, self.send, self.recv = src, dst, send, recv

        def copy(self, i):
            to = chan_at(i)
            return pltpu.make_async_remote_copy(
                src_ref=self.src(to), dst_ref=self.dst(c), send_sem=self.send.at[i],
                recv_sem=self.recv.at[i], device_id=(d, to), device_id_type=MESH,
            )

        def local(self):
            return pltpu.make_async_copy(self.src(c), self.dst(c), self.recv.at[0])

        def start(self):
            for i in (2, 1, 3) if nc == 4 else range(1, nc):
                self.copy(i).start()
            self.local().start()

        def wait(self):
            self.local().wait()
            for i in range(1, nc):
                frm = lax.rem(c - i + nc, nc)
                pltpu.make_async_remote_copy(
                    src_ref=self.src(c), dst_ref=self.dst(frm), send_sem=self.send.at[i],
                    recv_sem=self.recv.at[i], device_id=(d, frm), device_id_type=MESH,
                ).wait_recv()
                self.copy(i).wait_send()

    gs_sem, gr_sem = r.gather_send, r.gather_recv
    xs_sem, xr_sem = r.image_send, r.image_recv
    os_sem, or_sem = r.out_send, r.out_got

    def lanes_of(ref, width):
        return lambda s: ref.at[:, pl.ds(pl.multiple_of(s * width, LANES), width)]

    def rows_of(ref, size):
        return lambda s: ref.at[pl.ds(pl.multiple_of(s * size, size), size), :]

    def mids_of(ref, size):
        return lambda s: ref.at[:, pl.ds(pl.multiple_of(s * size, size), size), :]

    def taps_of(ref, size):
        return lambda s: ref.at[:, :, pl.ds(pl.multiple_of(s * size, size), size), :]

    whole = lambda ref: (lambda s: ref)
    ms = z.mids
    sem_rows = iter(range(13))

    def gathered(src, dst):
        e = next(sem_rows)
        return Exchange(src, dst, gs_sem.at[e], gr_sem.at[e])

    ex = SimpleNamespace(
        vec=gathered(whole(given.vec), lambda s: r.vv.at[s]),
        wsh=gathered(whole(given.wsh), lanes_of(r.wsh, z.cos)),
        cot=gathered(rows_of(given.cot, no), lanes_of(r.cot, z.cos)),
        blk={
            k: SimpleNamespace(
                wrt=gathered(whole(given.blk[k].wrt), rows_of(r.blk[k].wrt, ms)),
                wst=gathered(whole(given.blk[k].wst), taps_of(r.blk[k].wst, ms)),
                sq=gathered(whole(given.blk[k].sq), rows_of(r.blk[k].sq, ms)),
                ext=gathered(whole(given.blk[k].ext), mids_of(r.blk[k].ext, ms)),
                we=gathered(whole(given.blk[k].we), lanes_of(r.blk[k].we, z.cos)),
            )
            for k in (1, 2)
        },
        x=[],
    )
    nq = QUARTERS
    part = ni // nq
    for q in range(nq):
        ex.x.append(Exchange(
            lambda s, q=q: given.images.at[pl.ds(pl.multiple_of(s * ni + q * part, part), part), :],
            lambda s, q=q: r.x.at[
                pl.ds(q * part, part), pl.ds(pl.multiple_of(s * z.cis, LANES), z.cis)
            ],
            xs_sem.at[q],
            xr_sem.at[q],
        ))
    ex.blk[1].wrt.start()
    ex.vec.start()
    ex.x[0].start()
    ex.wsh.start()
    for q in range(1, nq):
        ex.x[q].start()
    for k in (1, 2):
        w = ex.blk[k]
        for e in ((w.wst, w.sq, w.ext, w.we) if k == 1 else (w.wrt, w.wst, w.sq, w.ext, w.we)):
            e.start()
    ex.cot.start()

    ss0, rs0, ss1, rs1 = r.s0s, r.s0r, r.s1s, r.s1r

    def put(k, row, v):
        for t in range(v.shape[1] // LANES):
            r.sync[k].sa[row + t : row + t + 1, :] = v[:, t * LANES : (t + 1) * LANES]

    def allreduce(k, used, meanwhile=None):
        sa, sb, st = r.sync[k].sa, r.sync[k].sb, r.sync[k].st
        rows = SYNC_ROWS[k]
        sc = r.slots[k % 2].at[:, :rows, :]
        if used < rows:
            sa[used:rows, :] = jnp.zeros((rows - used, LANES), F32)
        first = pltpu.make_async_remote_copy(
            src_ref=sa, dst_ref=sb, send_sem=ss0.at[0], recv_sem=rs0.at[k % 2],
            device_id=partner, device_id_type=MESH,
        )
        first.start()
        first.wait()
        pair = sa[...] + sb[...]
        sc[me] = pair

        def send(i, _):
            j = lax.rem(i + ns // 3, ns - 1) + 1
            pltpu.make_async_remote_copy(
                src_ref=sc.at[me], dst_ref=sc.at[me], send_sem=ss1.at[j],
                recv_sem=rs1.at[k % 2, me], device_id=place(lax.rem(me + j, ns)),
                device_id_type=MESH,
            ).start()
            return 0

        lax.fori_loop(0, ns - 1, send, 0)

        if meanwhile is not None:
            meanwhile()

        def arrive(j, _):
            s = lax.rem(me + j, ns)
            pltpu.make_async_remote_copy(
                src_ref=sc.at[me], dst_ref=sc.at[s], send_sem=ss1.at[j],
                recv_sem=rs1.at[k % 2, s], device_id=place(s), device_id_type=MESH,
            ).wait()
            return 0

        lax.fori_loop(1, ns, arrive, 0)
        if ns <= 16:
            total = sc[0]
            for s in range(1, ns):
                total = total + sc[s]
        else:
            total = lax.fori_loop(1, ns, lambda s, t: t + sc[s], sc[0])
        st[...] = total

    def total(k, row, width):
        st = r.sync[k].st
        return jnp.concatenate(
            [st[row + t : row + t + 1, :] for t in range(width // LANES)], axis=1
        )

    sto = made.sto

    def keep(row, v):
        for t in range(v.shape[1] // LANES):
            sto[row + t : row + t + 1, :] = v[:, t * LANES : (t + 1) * LANES]

    half = lambda rows: lax.broadcasted_iota(jnp.int32, (rows, LANES), 0)
    groups = given.groups
    sides = [(so - 4 + 2 * groups[c * b + k]) for k in range(b)]
    areas = [(s * s).astype(F32) for s in sides]
    for k in range(b):
        def fill_out(t, _, k=k):
            p = half(2 * so) + t * (2 * so)
            ok = (lax.div(p, so) < sides[k]) & (lax.rem(p, so) < sides[k])
            r.mo[span(k * po + t * (2 * so), 2 * so), :] = jnp.where(ok, 1.0, 0.0)
            return 0

        lax.fori_loop(0, po // (2 * so), fill_out, 0)

        def fill_in(t, _, k=k):
            p = half(2 * si) + t * (2 * si)
            ok = (lax.div(p, si) < 2 * sides[k]) & (lax.rem(p, si) < 2 * sides[k])
            r.mi[span(k * pi_ + t * (2 * si), 2 * si), :] = jnp.where(ok, 1.0, 0.0).astype(BF16)
            return 0

        lax.fori_loop(0, pi_ // (2 * si), fill_in, 0)
    row8 = lax.broadcasted_iota(jnp.int32, (8, LANES), 0)
    live8 = jnp.where(row8 < b, 1.0, 0.0)
    inv_area = jnp.zeros((8, LANES), F32)
    for k in range(b):
        inv_area = jnp.where(row8 == k, 1.0 / jnp.full((8, LANES), areas[k], F32), inv_area)
    for ref in (r.blk[1].pm, r.blk[2].pm, r.ags):
        ref[...] = jnp.zeros_like(ref)

    pool_rows = part // 4

    def pool_matrix(out_axis):
        shape = (pool_rows, part) if out_axis == 0 else (part, pool_rows)
        o = lax.broadcasted_iota(jnp.int32, shape, out_axis)
        p = lax.broadcasted_iota(jnp.int32, shape, 1 - out_axis)
        row, col = lax.div(p, si), lax.rem(p, si)
        hit = (lax.div(row, 2) * so + lax.div(col, 2)) == o
        return jnp.where(hit, 0.25, 0.0).astype(BF16)

    low_half = lax.broadcasted_iota(jnp.int32, (1, LANES), 1) < z.mids
    vv = r.vv

    def v_mid(row):
        return jnp.concatenate(
            [
                jnp.where(low_half, vv[s, row : row + 1, :], vv[s + 1, row : row + 1, :])
                for s in range(0, nc, 2)
            ],
            axis=1,
        )

    def v_split(row):
        return jnp.concatenate([v_mid(row), v_mid(row + 1)], axis=1)

    def v_co(row):
        return jnp.concatenate(
            [
                vv[s, row + t : row + t + 1, :]
                for s in range(nc)
                for t in range(z.cos // LANES)
            ],
            axis=1,
        )

    def norm(k, row1, row2, width, inv_n, gain, bias):
        n = tiled(inv_n, width)
        mean = total(k, row1, width) * n
        inv = lax.rsqrt(total(k, row2, width) * n - mean * mean + EPSILON)
        scale = gain * inv
        return SimpleNamespace(mean=mean, inv=inv, gs=scale, sh=bias - mean * scale)

    def norm_grad(k, rowu, rowv, width, inv_n, nm):
        n = tiled(inv_n, width)
        su = total(k, rowu, width)
        sux = nm.inv * (total(k, rowv, width) - nm.mean * su)
        t = sux * n
        return (
            su,
            sux,
            nm.gs * (su * n - nm.mean * nm.inv * t),
            nm.gs * nm.inv * t,
        )

    def loop(n, tile, body, init):
        def step(i, carry):
            return body(pl.multiple_of(i * tile, tile), carry)

        return lax.fori_loop(0, n // tile, step, init)

    def zero8(width):
        return jnp.zeros((8, width), F32)

    def moments(ref, rows, width, tile):
        def body(at, carry):
            s1, s2 = carry
            v = ref[pl.ds(at, tile), :]
            mv = v * tiled(r.mo[pl.ds(at, tile), :], width)
            return s1 + sum8(mv), s2 + sum8(mv * v)

        s1, s2 = loop(rows, tile, body, (zero8(width), zero8(width)))
        return fold(s1), fold(s2)

    red1 = r.red1

    def row_pair(ref, i):
        return jnp.concatenate(
            [ref[t, pl.ds(i, 1)].reshape(2 * si, LANES) for t in range(mid // LANES)], axis=1
        )

    def phase_of(t, lead, p, q):
        return red1[t, lead, p, pl.ds(q, so, stride=2), :].reshape(4 * so, LANES)

    pool_m = pool_matrix(0)
    ex.blk[1].wrt.wait()
    r1, r2 = zero8(mid), zero8(mid)
    for q in range(nq):
        ex.x[q].wait()
        xv = r.x[q * part : (q + 1) * part, :]
        lead = part // (2 * si)
        reduced = dot(xv, r.blk[1].wrt[...], NT)
        for t in range(mid // LANES):
            red1[t, q * lead : (q + 1) * lead] = reduced[:, t * LANES : (t + 1) * LANES].reshape(
                lead, 2, si, LANES
            )

        def red_sums(i, carry, q=q, lead=lead):
            s1, s2 = carry
            v = row_pair(red1, q * lead + i)
            m = r.mi[span((q * lead + i) * 2 * si, 2 * si), :].astype(F32)
            mv = v * tiled(m, mid)
            return s1 + sum8(mv), s2 + sum8(mv * v)

        r1, r2 = lax.fori_loop(0, lead, red_sums, (r1, r2))
        pooled = dot(pool_m, xv).astype(BF16)
        r.pool[q * pool_rows : (q + 1) * pool_rows, :] = pooled
    ex.wsh.wait()
    for n0 in range(0, co, 256):
        r.short[:, n0 : n0 + 256] = dot(r.pool[...], r.wsh[:, n0 : n0 + 256])
    h1, h2 = moments(r.short, no, co, 16)
    put(0, 0, fold(r1))
    put(0, mid // LANES, fold(r2))
    at = 2 * mid // LANES
    put(0, at, h1)
    put(0, at + co // LANES, h2)
    local_area = areas[0]
    for k in range(1, b):
        local_area = local_area + areas[k]
    put(0, at + 2 * co // LANES, jnp.full((1, LANES), local_area, F32))
    allreduce(0, at + 2 * co // LANES + 1)
    ex.vec.wait()
    count = total(0, at + 2 * co // LANES, LANES)
    inv_out = 1.0 / count
    inv_in = 0.25 * inv_out
    vr1, vr2 = VEC_ROWS[1], VEC_ROWS[2]
    nred1 = norm(0, 0, mid // LANES, mid, inv_in, v_mid(vr1.rg), v_mid(vr1.rb))
    nshort = norm(0, at, at + co // LANES, co, inv_out, v_co(vr1.hg), v_co(vr1.hb))

    lane16 = lax.rem(lax.broadcasted_iota(jnp.int32, (4 * so, mid), 0), so)
    not_first = lane16 > 0
    not_last = lane16 < so - 1

    def im_put(im, at, w, di, dj, shift):
        tap = di * 3 + dj
        low = w.astype(BF16)
        for g in range(2):
            im[g, pl.ds(pl.multiple_of(at + so + shift * so, so), 4 * so), tap * grp : (tap + 1) * grp] = (
                low[:, g * grp : (g + 1) * grp]
            )

    def im_zero(im, di, last):
        for k in range(b):
            row = so + k * po + (po - so if last else 0)
            for g in range(2):
                im[g, row : row + so, di * 3 * grp : (di + 1) * 3 * grp] = jnp.zeros(
                    (so, 3 * grp), BF16
                )

    im1 = r.blk[1].im

    def build1(i, _):
        at = pl.multiple_of(i * 4 * so, 4 * so)
        m = tiled(r.mo[pl.ds(at, 4 * so), :], mid)
        for p in range(2):
            for q in range(2):
                v = jnp.concatenate(
                    [phase_of(t, pl.ds(i * 4, 4), p, q) for t in range(mid // LANES)], axis=1
                )
                w = silu(v * nred1.gs + nred1.sh) * m
                for dj in ((1,) if q == 0 else (2, 0)):
                    wj = w
                    if dj == 0:
                        wj = jnp.where(not_first, pltpu.roll(w, 1, 0), 0.0)
                    for di in ((1,) if p == 0 else (2, 0)):
                        im_put(im1, at, wj, di, dj, 1 if di == 0 else 0)
        return 0

    lax.fori_loop(0, no // (4 * so), build1, 0)
    im_zero(im1, 0, False)

    def split_weights(k, g):
        return jnp.concatenate([r.blk[k].wst[t, g] for t in range(TAPS)], axis=1)

    def split_conv(k):
        ex.blk[k].wst.wait()
        for g in range(2):
            r.blk[k].sp[:, g * mid : (g + 1) * mid] = dot(
                r.blk[k].im[g, so : so + no, :], split_weights(k, g), NT
            )
        return moments(r.blk[k].sp, no, 2 * mid, 32)

    def attention_forward(k, vr, sync):
        s1, s2 = split_conv(k)
        put(sync, 0, s1)
        put(sync, 4, s2)
        allreduce(sync, 8)
        nsplit = norm(sync, 0, 4, 2 * mid, inv_out, v_split(vr.sg), v_split(vr.sb))
        sp, sa, pm = r.blk[k].sp, r.blk[k].sa, r.blk[k].pm
        for img in range(b):
            def act(at, s, img=img):
                rows = pl.ds(pl.multiple_of(at + img * po, 32), 32)
                v = silu(sp[rows, :] * nsplit.gs + nsplit.sh)
                v = v * tiled(r.mo[rows, :], 2 * mid)
                sa[rows, :] = v
                return s + sum8(v)

            s = fold(loop(po, 32, act, zero8(2 * mid)))
            pm[img : img + 1, :] = (s[:, :mid] + s[:, mid:]) * tiled(inv_area[img : img + 1, :], mid)
        ex.blk[k].sq.wait()
        squeezed = dot_exact(pm[...], r.blk[k].sq[...])
        put(sync + 1, 0, fold(squeezed))
        put(sync + 1, 1, fold(squeezed * squeezed))
        put(sync + 1, 2, fold(pm[...]))
        allreduce(sync + 1, 4)
        inv_images = jnp.full((1, LANES), 1.0 / (b * nc * nd), F32)
        natt = norm(
            sync + 1, 0, 1, att, inv_images, vv[0, vr.qg : vr.qg + 1, :],
            vv[0, vr.qb : vr.qb + 1, :],
        )
        xhat = (squeezed - natt.mean) * natt.inv
        centred = pm[...] - total(sync + 1, 2, mid) * tiled(inv_images, mid)
        pre = squeezed * natt.gs + natt.sh
        excited = silu(pre) * live8
        ex.blk[k].ext.wait()
        halves = []
        for g in range(2):
            bias = v_mid(vr.xb + g)
            halves.append(dot_exact(excited, r.blk[k].ext[g], NT) + bias)
        top = jnp.maximum(halves[0], halves[1])
        e0, e1 = jnp.exp(halves[0] - top), jnp.exp(halves[1] - top)
        whole_sum = e0 + e1
        at_ref = r.blk[k].att
        at_ref[:, :mid] = e0 / whole_sum
        at_ref[:, mid:] = e1 / whole_sum
        for img in range(b):
            def mix(at, _, img=img):
                rows = pl.ds(pl.multiple_of(at + img * po, 32), 32)
                v = sa[rows, :] * at_ref[img : img + 1, :]
                r.blk[k].mix[rows, :] = (v[:, :mid] + v[:, mid:]).astype(BF16)
                return 0

            loop(po, 32, mix, 0)
        ex.blk[k].we.wait()
        for n0 in range(0, co, 256):
            r.blk[k].exp[:, n0 : n0 + 256] = dot(r.blk[k].mix[...], r.blk[k].we[:, n0 : n0 + 256])
        s1, s2 = moments(r.blk[k].exp, no, co, 16)
        put(sync + 2, 0, s1)
        put(sync + 2, co // LANES, s2)
        allreduce(sync + 2, 2 * co // LANES)
        nexp = norm(sync + 2, 0, co // LANES, co, inv_out, v_co(vr.eg), v_co(vr.eb))
        return SimpleNamespace(nsplit=nsplit, natt=natt, xhat=xhat, pre=pre, excited=excited, nexp=nexp, centred=centred)

    f1 = attention_forward(1, vr1, 1)

    def summed1(rows):
        return (
            r.blk[1].exp[rows, :] * f1.nexp.gs
            + f1.nexp.sh
            + r.short[rows, :] * nshort.gs
            + nshort.sh
        )

    def hidden(at, _):
        rows = pl.ds(at, 16)
        r.h[rows, :] = (silu(summed1(rows)) * tiled(r.mo[rows, :], co)).astype(BF16)
        return 0

    loop(no, 16, hidden, 0)

    ex.blk[2].wrt.wait()
    r.red2[...] = dot(r.h[...], r.blk[2].wrt[...], NT)
    s1, s2 = moments(r.red2, no, mid, 64)
    put(4, 0, s1)
    put(4, 2, s2)
    allreduce(4, 4)
    nred2 = norm(4, 0, 2, mid, inv_out, v_mid(vr2.rg), v_mid(vr2.rb))
    im2 = r.blk[2].im

    def build2(i, _):
        at = pl.multiple_of(i * 4 * so, 4 * so)
        m = tiled(r.mo[pl.ds(at, 4 * so), :], mid)
        w = silu(r.red2[pl.ds(at, 4 * so), :] * nred2.gs + nred2.sh) * m
        for dj in range(3):
            wj = w
            if dj == 0:
                wj = jnp.where(not_first, pltpu.roll(w, 1, 0), 0.0)
            if dj == 2:
                wj = jnp.where(not_last, pltpu.roll(w, 4 * so - 1, 0), 0.0)
            for di in range(3):
                im_put(im2, at, wj, di, dj, 1 - di)
        return 0

    lax.fori_loop(0, no // (4 * so), build2, 0)
    im_zero(im2, 0, False)
    im_zero(im2, 2, True)
    f2 = attention_forward(2, vr2, 5)

    ex.cot.wait()

    def finish(at, carry):
        su, sv = carry
        rows = pl.ds(at, 16)
        m = tiled(r.mo[rows, :], co)
        v = r.blk[2].exp[rows, :]
        s = v * f2.nexp.gs + f2.nexp.sh + r.h[rows, :].astype(F32)
        q = sigmoid(s)
        u = r.cot[rows, :].astype(F32) * m * (q * (1.0 + s * (1.0 - q)))
        r.cot[rows, :] = (s * q * m).astype(BF16)
        r.g[rows, :] = u
        return su + sum8(u), sv + sum8(u * v)

    su, sv = loop(no, 16, finish, (zero8(co), zero8(co)))
    out_ex = Exchange(
        lambda s: r.cot.at[:, pl.ds(pl.multiple_of(s * z.cos, LANES), z.cos)],
        lambda s: made.out.at[pl.ds(pl.multiple_of(s * no, no), no), :],
        os_sem.at[0],
        or_sem.at[0],
    )
    out_ex.start()
    put(8, 0, fold(su))
    put(8, co // LANES, fold(sv))
    allreduce(8, 2 * co // LANES)

    def pack_rows(k, name, skip, v):
        group, at = z.lay[(k, name)]
        at, share = at + skip * z.mids, z.mids
        for s in range(nc):
            for t in range(v.shape[1] // LANES):
                r.group[group].pk[s // 2, s % 2, at + t * share : at + (t + 1) * share, :] = v[
                    s * share : (s + 1) * share, t * LANES : (t + 1) * LANES
                ].astype(BF16)

    def pack_lanes(k, name, s, v):
        group, at = z.lay[(k, name)]
        rows = v.shape[0]
        for t in range(v.shape[1] // LANES):
            r.group[group].pk[s // 2, s % 2, at + t * rows : at + (t + 1) * rows, :] = v[
                :, t * LANES : (t + 1) * LANES
            ].astype(BF16)

    class Reduction:
        def __init__(self, group):
            own = r.group[group]
            self.pk, self.r1, self.r2, self.r3 = own.pk, own.r1, own.r2, own.r3
            self.rows = z.rows[group]
            self.piece = self.rows // nd
            self.res = made.res[group]
            self.sems = [own.q1, own.q2, own.q3s, own.q3r, own.q4s, own.q4r]
            self.across = lax.div(c, 2)

        def piece_at(self, n):
            return pl.ds(pl.multiple_of(n * self.piece, 16), self.piece)

        def copy1(self):
            return pltpu.make_async_remote_copy(
                src_ref=self.pk.at[:, 1 - odd], dst_ref=self.r1, send_sem=self.sems[0].at[0],
                recv_sem=self.sems[0].at[1], device_id=partner, device_id_type=MESH,
            )

        def copy2(self):
            return pltpu.make_async_remote_copy(
                src_ref=self.pk.at[1 - self.across, odd], dst_ref=self.r2,
                send_sem=self.sems[1].at[0], recv_sem=self.sems[1].at[1],
                device_id=(d, chan_at(2)), device_id_type=MESH,
            )

        def copy3(self, to, src):
            return pltpu.make_async_remote_copy(
                src_ref=self.pk.at[self.across, odd, self.piece_at(to), :],
                dst_ref=self.r3.at[src], send_sem=self.sems[2].at[to],
                recv_sem=self.sems[3].at[src], device_id=(to, c), device_id_type=MESH,
            )

        def copy4(self, to, src):
            return pltpu.make_async_remote_copy(
                src_ref=self.r3.at[d], dst_ref=self.res.at[self.piece_at(src), :],
                send_sem=self.sems[4].at[to], recv_sem=self.sems[5].at[src],
                device_id=(to, c), device_id_type=MESH,
            )

        def local4(self):
            return pltpu.make_async_copy(
                self.r3.at[d], self.res.at[self.piece_at(d), :], self.sems[5].at[d]
            )

        def add(self, which, other):
            def body(at, _):
                rows = pl.ds(at, 128)
                self.pk[which, odd, rows, :] = (
                    self.pk[which, odd, rows, :].astype(F32) + other(rows).astype(F32)
                ).astype(BF16)
                return 0

            loop(self.rows, 128, body, 0)

        def step1(self):
            self.copy1().start()

        def step2(self):
            self.copy1().wait()
            away = 1 - self.across
            self.add(away, lambda rows: self.r1[away, rows, :])
            self.copy2().start()
            self.add(self.across, lambda rows: self.r1[self.across, rows, :])

        def step3(self):
            self.copy2().wait_recv()
            self.add(self.across, lambda rows: self.r2[rows, :])

            def send(j, _):
                self.copy3(lax.rem(d + j, nd), d).start()
                return 0

            lax.fori_loop(1, nd, send, 0)
            self.copy2().wait_send()

        def step4(self):
            self.r3[d] = self.pk[self.across, odd, self.piece_at(d), :]

            def arrive(j, _):
                to, src = lax.rem(d + j, nd), lax.rem(d - j + nd, nd)
                self.copy3(to, d).wait_send()
                self.copy3(src, src).wait_recv()
                return 0

            lax.fori_loop(1, nd, arrive, 0)

            def body(at, _):
                rows = pl.ds(at, 16)

                def term(n, t):
                    return t + self.r3[n, rows, :].astype(F32)

                t = self.r3[0, rows, :].astype(F32)
                if nd <= 8:
                    for n in range(1, nd):
                        t = term(n, t)
                else:
                    t = lax.fori_loop(1, nd, term, t)
                self.r3[d, rows, :] = t.astype(BF16)
                return 0

            loop(self.piece, 16, body, 0)
            self.local4().start()

            def send(j, _):
                self.copy4(lax.rem(d + j, nd), d).start()
                return 0

            lax.fori_loop(1, nd, send, 0)

        def finish(self):
            self.local4().wait()

            def arrive(j, _):
                to, src = lax.rem(d + j, nd), lax.rem(d - j + nd, nd)
                self.copy4(to, d).wait_send()
                self.copy4(src, src).wait_recv()
                return 0

            lax.fori_loop(1, nd, arrive, 0)

    sums_of = {group: Reduction(group) for group in GROUPS}

    def attention_backward(k, f, sync):
        srow = STO_ROWS[k]
        nexp, nsplit, natt = f.nexp, f.nsplit, f.natt
        first = k == 1
        cw = co // LANES
        su, sux, ea, eb = norm_grad(sync, 0, cw, co, inv_out, nexp)
        keep(srow.eb, su)
        keep(srow.eg, sux)
        if first:
            _, suxh, ha, hb = norm_grad(sync, 0, 2 * cw, co, inv_out, nshort)
            keep(srow.hg, suxh)

        def expand_grad(at, _):
            rows = pl.ds(at, 16)
            m = tiled(r.mo[rows, :], co)
            u = r.g[rows, :]
            r.eg[rows, :] = (nexp.gs * u - m * (ea + eb * r.blk[k].exp[rows, :])).astype(BF16)
            if first:
                r.shg[rows, :] = (
                    nshort.gs * u - m * (ha + hb * r.short[rows, :])
                ).astype(BF16)
            return 0

        loop(no, 16, expand_grad, 0)
        r.mg[...] = dot(r.eg[...], r.blk[k].we[...], NT)
        sa = r.blk[k].sa
        for img in range(b):
            def att_grad(at, s, img=img):
                rows = pl.ds(pl.multiple_of(at + img * po, 32), 32)
                return s + sum8(sa[rows, :] * tiled_pair(r.mg[rows, :]))

            r.ags[img : img + 1, :] = fold(loop(po, 32, att_grad, zero8(2 * mid)))
        ags, at_ref = r.ags, r.blk[k].att
        a0, a1 = at_ref[:, :mid], at_ref[:, mid:]
        g0, g1 = ags[:, :mid], ags[:, mid:]
        mean = a0 * g0 + a1 * g1
        l0, l1 = a0 * (g0 - mean), a1 * (g1 - mean)
        ext = r.blk[k].ext
        excited_grad = dot_exact(l0, ext[0]) + dot_exact(l1, ext[1])
        au = excited_grad * silu_slope(f.pre)
        put(sync + 1, 0, fold(au))
        put(sync + 1, 1, fold(au * f.xhat))
        put(sync + 1, 2, fold(l0))
        put(sync + 1, 4, fold(l1))

        def matrices():
            r.mixt[...] = jnp.transpose(r.blk[k].mix[...])
            for s in range(nc):
                share = slice(s * z.cos, (s + 1) * z.cos)
                pack_lanes(k, EXPAND, s, dot(r.mixt[...], r.eg[:, share]))
            pack_rows(k, EXCITE, 0, dot_exact(l0, f.excited, TN))
            pack_rows(k, EXCITE, 1, dot_exact(l1, f.excited, TN))
            if first:
                r.sgt[...] = jnp.transpose(r.pool[...])
                for s in range(nc):
                    share = slice(s * z.cos, (s + 1) * z.cos)
                    pack_lanes(k, SHORTCUT, s, dot(r.sgt[...], r.shg[:, share]))
                sums_of[1].step1()
                r.pg[...] = dot(r.shg[...], r.wsh[...], NT).astype(BF16)

        allreduce(sync + 1, 6, matrices)
        inv_images = 1.0 / (b * nc * nd)
        su, sux = total(sync + 1, 0, att), total(sync + 1, 1, att)
        keep(srow.qb, su)
        keep(srow.qg, sux)
        keep(srow.xb, total(sync + 1, 2, 2 * mid))
        sb = natt.gs * (au - su * inv_images - f.xhat * (sux * inv_images)) * live8
        if first:
            sums_of[0].step3()
            sums_of[1].step2()
        r.mgr[...] = dot_exact(sb, r.blk[k].sq[...], NT) * tiled(inv_area, mid)
        sp = r.blk[k].sp
        carry = (zero8(2 * mid), zero8(2 * mid))
        for img in range(b):
            def split_up(at, carry, img=img):
                s1, s2 = carry
                rows = pl.ds(pl.multiple_of(at + img * po, 32), 32)
                m = tiled(r.mo[rows, :], 2 * mid)
                v = sp[rows, :]
                grad = tiled_pair(r.mg[rows, :]) * at_ref[img : img + 1, :] + tiled_pair(
                    r.mgr[img : img + 1, :]
                )
                u = grad * m * silu_slope(v * nsplit.gs + nsplit.sh)
                r.su[rows, :] = u
                return s1 + sum8(u), s2 + sum8(u * v)

            carry = loop(po, 32, split_up, carry)
        put(sync + 2, 0, fold(carry[0]))
        put(sync + 2, 4, fold(carry[1]))

        def squeeze_matrix():
            pack_rows(k, SQUEEZE, 0, dot_exact(f.centred, sb, TN))

        allreduce(sync + 2, 8, squeeze_matrix)
        su, sux, ca, cb = norm_grad(sync + 2, 0, 4, 2 * mid, inv_out, nsplit)
        keep(srow.sb, su)
        keep(srow.sg, sux)

        def split_grad(at, _):
            rows = pl.ds(at, 32)
            m = tiled(r.mo[rows, :], 2 * mid)
            r.sgb[rows, :] = (
                nsplit.gs * r.su[rows, :] - m * (ca + cb * sp[rows, :])
            ).astype(BF16)
            return 0

        loop(no, 32, split_grad, 0)

    def tiled_pair(v):
        return jnp.concatenate([v, v], axis=1)

    def split_matrix(k):
        r.sgt[...] = jnp.transpose(r.sgb[...])
        for g in range(2):
            for t in range(3):
                v = dot(
                    r.sgt[g * mid : (g + 1) * mid, :],
                    r.blk[k].im[g, so : so + no, 3 * t * grp : 3 * (t + 1) * grp],
                )
                for u in range(3):
                    pack_rows(
                        k, SPLIT, (3 * t + u) * 2 + g, v[:, u * grp : (u + 1) * grp]
                    )

    dcol = r.dcol
    dcol[:so, :] = jnp.zeros((so, kk), F32)
    dcol[so + po :, :] = jnp.zeros((so, kk), F32)

    def columns(k, img, g):
        dcol[so : so + po, :] = dot(
            r.sgb[img * po : (img + 1) * po, g * mid : (g + 1) * mid], split_weights(k, g)
        )

    tile = 4 * so
    first_g, last_g = not_first[:, :grp], not_last[:, :grp]

    def tap(at, di, dj, shift):
        t = di * 3 + dj
        return dcol[pl.ds(pl.multiple_of(at + so - shift * so, so), tile), t * grp : (t + 1) * grp]

    def from_left(v):
        return jnp.where(first_g, pltpu.roll(v, 1, 0), 0.0)

    def from_right(v):
        return jnp.where(last_g, pltpu.roll(v, tile - 1, 0), 0.0)

    attention_backward(2, f2, 8)
    sums = []
    for g in range(2):
        carry = (zero8(grp), zero8(grp))
        lanes = slice(g * grp, (g + 1) * grp)
        for img in range(b):
            columns(2, img, g)

            def back2(at, carry, img=img, g=g, lanes=lanes):
                s1, s2 = carry
                cols = [
                    tap(at, 0, dj, -1) + tap(at, 1, dj, 0) + tap(at, 2, dj, 1) for dj in range(3)
                ]
                grad = cols[1] + from_right(cols[0]) + from_left(cols[2])
                rows = pl.ds(pl.multiple_of(at + img * po, tile), tile)
                v = r.red2[rows, lanes]
                u = (
                    grad
                    * tiled(r.mo[rows, :], grp)
                    * silu_slope(v * nred2.gs[:, lanes] + nred2.sh[:, lanes])
                )
                r.u2[rows, lanes] = u
                return s1 + sum8(u), s2 + sum8(u * v)

            carry = loop(po, tile, back2, carry)
        sums.append(carry)
    put(11, 0, jnp.concatenate([fold(s[0]) for s in sums], axis=1))
    put(11, 2, jnp.concatenate([fold(s[1]) for s in sums], axis=1))
    allreduce(11, 4, lambda: split_matrix(2))
    su, sux, ca, cb = norm_grad(11, 0, 2, mid, inv_out, nred2)
    keep(STO_ROWS[2].rb, su)
    keep(STO_ROWS[2].rg, sux)

    def reduce_grad2(at, _):
        rows = pl.ds(at, 64)
        m = tiled(r.mo[rows, :], mid)
        r.rg1[rows, :] = (
            nred2.gs * r.u2[rows, :] - m * (ca + cb * r.red2[rows, :])
        ).astype(BF16)
        return 0

    loop(no, 64, reduce_grad2, 0)
    for n0 in range(0, co, 256):
        cols = slice(n0, n0 + 256)
        r.g[:, cols] = r.g[:, cols] + dot(r.rg1[:no, :], r.blk[2].wrt[:, cols])

    def first_up(at, carry):
        s1, s2, s3 = carry
        rows = pl.ds(at, 16)
        u = r.g[rows, :] * tiled(r.mo[rows, :], co) * silu_slope(summed1(rows))
        r.g[rows, :] = u
        return (
            s1 + sum8(u),
            s2 + sum8(u * r.blk[1].exp[rows, :]),
            s3 + sum8(u * r.short[rows, :]),
        )

    s1, s2, s3 = loop(no, 16, first_up, (zero8(co), zero8(co), zero8(co)))
    put(12, 0, fold(s1))
    put(12, co // LANES, fold(s2))
    put(12, 2 * co // LANES, fold(s3))

    def reduce_matrix2():
        r.rgt[:, :no] = jnp.transpose(r.rg1[:no, :])
        for n0 in range(0, co, 256):
            pack_rows(2, REDUCE, n0 // LANES, dot(r.rgt[:, :no], r.h[:, n0 : n0 + 256]))
        sums_of[0].step1()

    allreduce(12, 3 * co // LANES, reduce_matrix2)
    sums_of[0].step2()

    attention_backward(1, f1, 12)
    sums = []
    for g in range(2):
        carry = (zero8(grp), zero8(grp))
        lanes = slice(g * grp, (g + 1) * grp)
        for img in range(b):
            columns(1, img, g)

            def back1(at, carry, img=img, g=g, lanes=lanes):
                s1, s2 = carry
                rows = pl.ds(pl.multiple_of(at + img * po, tile), tile)
                m = tiled(r.mo[rows, :], grp)
                lead = pl.ds(pl.multiple_of(lax.div(at, so) + img * so, 4), 4)
                for p in range(2):
                    for q in range(2):
                        def col(dj):
                            if p == 0:
                                return tap(at, 1, dj, 0)
                            return tap(at, 0, dj, -1) + tap(at, 2, dj, 0)

                        grad = col(1) if q == 0 else col(2) + from_right(col(0))
                        v = phase_of(g, lead, p, q)
                        u = grad * m * silu_slope(v * nred1.gs[:, lanes] + nred1.sh[:, lanes])
                        r.u1[g, lead, p, pl.ds(q, so, stride=2), :] = u.reshape(4, so, grp)
                        s1, s2 = s1 + sum8(u), s2 + sum8(u * v)
                return s1, s2

            carry = loop(po, tile, back1, carry)
        sums.append(carry)
    put(15, 0, jnp.concatenate([fold(s[0]) for s in sums], axis=1))
    put(15, 2, jnp.concatenate([fold(s[1]) for s in sums], axis=1))

    def split_matrix1():
        split_matrix(1)
        sums_of[2].step1()

    allreduce(15, 4, split_matrix1)
    sums_of[0].step4()
    sums_of[2].step2()
    su, sux, ca, cb = norm_grad(15, 0, 2, mid, inv_in, nred1)
    keep(STO_ROWS[1].rb, su)
    keep(STO_ROWS[1].rg, sux)

    def reduce_grad1(i, _):
        rows = pl.ds(pl.multiple_of(i * 2 * si, 2 * si), 2 * si)
        m = tiled(r.mi[rows, :].astype(F32), mid)
        u, v = row_pair(r.u1, i), row_pair(red1, i)
        r.rg1[rows, :] = (nred1.gs * u - m * (ca + cb * v)).astype(BF16)
        return 0

    lax.fori_loop(0, b * so, reduce_grad1, 0)
    r.rgt[...] = jnp.transpose(r.rg1[...])
    for n0 in range(0, ci, 256):
        pack_rows(1, REDUCE, n0 // LANES, dot(r.rgt[...], r.x[:, n0 : n0 + 256]))
    sums_of[3].step1()
    sums_of[1].step3()
    spread = pool_matrix(1)
    last = []
    for q in range(nq):
        rows = slice(q * part, (q + 1) * part)
        m = tiled(r.mi[rows, :].astype(F32), 256)
        for n0 in range(0, ci, 256):
            cols = slice(n0, n0 + 256)
            v = dot(r.rg1[rows, :], r.blk[1].wrt[:, cols]) + dot(
                spread, r.pg[q * pool_rows : (q + 1) * pool_rows, cols]
            )
            r.x[rows, cols] = (v * m).astype(BF16)
        e = Exchange(
            lambda s, q=q: r.x.at[
                pl.ds(q * part, part), pl.ds(pl.multiple_of(s * z.cis, LANES), z.cis)
            ],
            lambda s, q=q: made.gx.at[
                pl.ds(pl.multiple_of(s * ni + q * part, part), part), :
            ],
            os_sem.at[1 + q],
            or_sem.at[1 + q],
        )
        e.start()
        last.append(e)
    sums_of[3].step2()
    sums_of[2].step3()
    sums_of[1].step4()
    sums_of[3].step3()
    sums_of[2].step4()
    sums_of[3].step4()
    out_ex.wait()
    for e in last:
        e.wait()
    for sums in (sums_of[0], sums_of[1], sums_of[2], sums_of[3]):
        sums.finish()


class Weights:
    def __init__(self, values):
        (
            self.reduce, self.reducegain, self.reducebias,
            self.split, self.splitgain, self.splitbias,
            self.squeeze, self.squeezegain, self.squeezebias,
            self.excite, self.excitebias,
            self.expand, self.expandgain, self.expandbias,
        ) = values[:14]
        self.extra = values[14:]


def doubled(v):
    return jnp.concatenate([v, v], axis=-1).reshape(-1, LANES)


def per_device(mesh, images, cotangent, groups, *weights):
    first, second = Weights(weights[:17]), Weights(weights[17:])
    z = Sizes(mesh, images, first.reduce, first.expand, first.squeeze)

    def vectors(w):
        parts = [
            doubled(w.reducegain[None]), doubled(w.reducebias[None]),
            doubled(w.splitgain), doubled(w.splitbias), doubled(w.excitebias),
        ]
        parts += [v.reshape(-1, LANES) for v in (w.expandgain, w.expandbias) + w.extra[1:]]
        return parts + [w.squeezegain.reshape(-1, LANES), w.squeezebias.reshape(-1, LANES)]

    def block(w):
        return dict(
            wrt=w.reduce.T,
            wst=jnp.transpose(w.split, (0, 1, 3, 4, 2)).reshape(TAPS, 2, z.mids, z.grp),
            sq=w.squeeze,
            ext=jnp.transpose(w.excite, (1, 2, 0)),
            we=w.expand,
        )

    inputs = dict(
        images=images.reshape(-1, z.cis),
        cot=cotangent.reshape(-1, z.cos),
        groups=groups,
        vec=jnp.concatenate(vectors(first) + vectors(second), axis=0),
        wsh=first.extra[0],
        blk={1: block(first), 2: block(second)},
    )
    in_specs = jax.tree.map(lambda v: pl.BlockSpec(memory_space=pl.ANY), inputs)
    in_specs.update(groups=pl.BlockSpec(memory_space=pltpu.SMEM))
    outs = dict(
        out=jax.ShapeDtypeStruct((z.nc * z.no, z.cos), BF16),
        gx=jax.ShapeDtypeStruct((z.nc * z.ni, z.cis), BF16),
        sto=jax.ShapeDtypeStruct((NSTO, LANES), F32),
        res={n: jax.ShapeDtypeStruct((rows, LANES), BF16) for n, rows in z.rows.items()},
    )
    out_specs = jax.tree.map(lambda v: pl.BlockSpec(memory_space=pl.ANY), outs)
    out_specs.update(sto=pl.BlockSpec(memory_space=pltpu.VMEM))
    scratch = scratch_tree(z)
    tree = jax.tree.structure((inputs, outs, scratch))
    results = pl.pallas_call(
        functools.partial(mega_kernel, z, tree),
        out_shape=jax.tree.leaves(outs),
        in_specs=jax.tree.leaves(in_specs),
        out_specs=jax.tree.leaves(out_specs),
        scratch_shapes=jax.tree.leaves(scratch),
        compiler_params=pltpu.CompilerParams(
            collective_id=0, has_side_effects=True, vmem_limit_bytes=62 << 20
        ),
        name="two_blocks",
    )(*jax.tree.leaves(inputs))
    return unpack(z, jax.tree.unflatten(jax.tree.structure(outs), results))


def unpack_kernel(z, plan, tree, *refs):
    given, (out_image, gx, *outs) = jax.tree.unflatten(tree, refs)
    given = space(given)
    out_in, gx_in, sto, res = given.out, given.gx, given.sto, given.res
    c = lax.axis_index(CHAN)
    out_image[...] = out_in[...].astype(F32)
    gx[...] = gx_in[...].astype(F32)

    def mid_share(row):
        v = sto[pl.ds(row + lax.div(c, 2), 1), :]
        return jnp.where(lax.rem(c, 2) == 0, v[:, : z.mids], v[:, z.mids :])

    @pl.when(pl.program_id(0) == 0)
    def _():
        for (kind, k, name), o in zip(plan, outs):
            if kind == MATRIX:
                group, at = z.lay[(k, name)]
                rows = o.shape[0]
                for t in range(o.shape[1] // LANES):
                    o[:, t * LANES : (t + 1) * LANES] = res[group][
                        at + t * rows : at + (t + 1) * rows, :
                    ].astype(F32)
                continue
            row = name
            if kind == MID_VECTOR:
                o[...] = mid_share(row)
            elif kind == PAIR_VECTOR:
                o[0:1, :] = mid_share(row)
                o[1:2, :] = mid_share(row + z.mid // LANES)
            elif kind == ATT_VECTOR:
                o[...] = sto[row : row + 1, :]
            else:
                n = z.cos // LANES
                for t in range(n):
                    o[:, t * LANES : (t + 1) * LANES] = sto[pl.ds(row + c * n + t, 1), :]


def unpack(z, results):
    plan = []
    for k in (1, 2):
        v = STO_ROWS[k]
        plan += [
            (MATRIX, k, REDUCE), (MID_VECTOR, k, v.rg), (MID_VECTOR, k, v.rb),
            (MATRIX, k, SPLIT), (PAIR_VECTOR, k, v.sg), (PAIR_VECTOR, k, v.sb),
            (MATRIX, k, SQUEEZE), (ATT_VECTOR, k, v.qg), (ATT_VECTOR, k, v.qb),
            (MATRIX, k, EXCITE), (PAIR_VECTOR, k, v.xb),
            (MATRIX, k, EXPAND), (OUT_VECTOR, k, v.eg), (OUT_VECTOR, k, v.eb),
        ]
        if k == 1:
            plan += [(MATRIX, k, SHORTCUT), (OUT_VECTOR, k, v.hg), (OUT_VECTOR, k, v.eb)]

    def shape_of(kind, k, name):
        if kind == MATRIX:
            return (
                (z.mids, z.ci if k == 1 else z.co),
                (2 * TAPS * z.mids, LANES),
                (z.mids, z.att),
                (2 * z.mids, z.att),
                (z.mid, z.cos),
                (z.ci, z.cos),
            )[name]
        return (None, (1, z.mids), (2, z.mids), (1, z.att), (1, z.cos))[kind]

    shapes = [shape_of(*entry) for entry in plan]
    steps = 8
    whole = lambda shape: pl.BlockSpec(shape, lambda i: (0, 0))
    slab = lambda v: pl.BlockSpec((v.shape[0] // steps, v.shape[1]), lambda i: (i, 0))
    in_specs = {n: slab(v) if n in ("out", "gx") else jax.tree.map(lambda a: whole(a.shape), v)
                for n, v in results.items()}
    images = [results["out"], results["gx"]]
    outs = [jax.ShapeDtypeStruct(v.shape, F32) for v in images]
    outs += [jax.ShapeDtypeStruct(s, F32) for s in shapes]
    flat = pl.pallas_call(
        functools.partial(unpack_kernel, z, plan, jax.tree.structure((results, outs))),
        grid=(steps,),
        out_shape=outs,
        in_specs=jax.tree.leaves(in_specs),
        out_specs=[slab(v) for v in images] + [whole(s) for s in shapes],
        compiler_params=pltpu.CompilerParams(vmem_limit_bytes=40 << 20),
        name="unpack",
    )(*jax.tree.leaves(results))
    final = [
        flat[0].reshape(z.nc * z.b, z.so, z.so, z.cos),
        flat[1].reshape(z.nc * z.b, z.si, z.si, z.cis),
    ]
    for (kind, _, name), v in zip(plan, flat[2:]):
        if (kind, name) == (MATRIX, REDUCE):
            v = v.T
        elif (kind, name) == (MATRIX, SPLIT):
            v = jnp.transpose(v.reshape(3, 3, 2, z.mids, z.grp), (0, 1, 4, 2, 3))
        elif (kind, name) == (MATRIX, EXCITE):
            v = jnp.transpose(v.reshape(2, z.mids, z.att), (2, 0, 1))
        elif kind in (MID_VECTOR, ATT_VECTOR, OUT_VECTOR):
            v = v.reshape(-1)
        final.append(v)
    return tuple(final)


def specs():
    block = [
        P(None, CHAN), P(CHAN), P(CHAN),
        P(None, None, None, None, CHAN), P(None, CHAN), P(None, CHAN),
        P(CHAN, None), P(), P(), P(None, None, CHAN), P(None, CHAN),
        P(None, CHAN), P(CHAN), P(CHAN),
    ]
    short = [P(None, CHAN), P(CHAN), P(CHAN)]
    return block + short + block


def solution(mesh):
    image = P(DP, None, None, CHAN)
    return jax.shard_map(
        functools.partial(per_device, mesh),
        mesh=mesh,
        in_specs=tuple([image, image, P(DP)] + specs()),
        out_specs=tuple([image, image] + specs()),
        check_vma=False,
    )
```

profile of v0, /device:TPU:0, one launch (start us, length us, event | category | flops | bytes accessed | tf_op | source)
XLA Modules:
  0.0 328.7 jit_solution(7518595150249826223)
XLA Ops:
  0.7 0.8 pad_maximum_fusion.6
  1.5 0.8 pad_maximum_fusion.8
  2.3 0.8 pad_maximum_fusion
  3.1 0.8 pad_maximum_fusion.2
  4.0 0.8 pad_maximum_fusion.4
  4.8 4.5 %concatenate.43.refs_13_ = f32[32,128]{1,0:T(8,128)} concatenate(f32[1,128]{1,0:T(1,128)S(1)} %get-tuple-element.119, f32[1,128]{1,0:T(1,128)S(1)} %get-tuple-element.120, f32[2,128]{1,0:T(2,128)S(1)} %get-tuple-element.113, f32[2,128]{1,0:T(2,128)S(1)} %get-tuple-element.114, f32[2,128]{1,0:T(2,128)S(1)} %get-tuple-element.115, f32[2,128]{1,0:T(2,128)} %bitcast.64, ...), dimensions={0} | concatenate | bytes 32768 | tf_op jit(solution)/shard_map/concatenate | solution.py:1243
  9.3 306.5 %two_blocks.1 = (bf16[8192,128]{1,0:T(8,128)(2,1)}, bf16[2048,256]{1,0:T(8,128)(2,1)}, bf16[2432,128]{1,0:T(8,128)(2,1)}, bf16[1664,128]{1,0:T(8,128)(2,1)}, bf1...) custom-call(bf16[2,64,128]{2,1,0:T(8,128)(2,1)} %bitcast.62, bf16[64,128]{1,0:T(8,128)(2,1)} %refs_1_.1, ...), custom_call_target="tpu_custom_call" | custom-call | tf_op jit(solution)/shard_map/two_blocks/pallas_call | solution.py:1259
  315.8 0.0 copy-start
  315.8 1.6 copy-done
  317.4 0.0 copy-start.1
  317.4 1.2 copy-done.1
  318.6 0.0 copy-start.2
  318.6 1.1 copy-done.2
  319.7 0.0 copy-start.3
  319.7 1.0 copy-done.3
  320.7 0.0 copy-start.4
  320.7 1.0 copy-done.4
  321.7 0.0 copy-start.5
  321.7 0.8 copy-done.5
  322.5 0.0 copy-start.6
  322.5 0.8 copy-done.6
  323.3 5.2 %unpack.1 = (f32[2048,256]{1,0:T(8,128)}, f32[8192,128]{1,0:T(8,128)}, f32[64,512]{1,0:T(8,128)}, f32[1,64]{1,0:T(1,128)}, f32[1,64]{1,0:T(1,128)}, /*index=5*/f...) custom-call(bf16[8192,128]{1,0:T(8,128)(2,1)S(1)} %copy-done, ...), custom_call_target="tpu_custom_call" | custom-call | tf_op jit(solution)/shard_map/unpack/pallas_call | solution.py:1345
Async XLA Ops:
  315.8 1.6 copy-start
  317.4 1.2 copy-start.1
  318.6 1.1 copy-start.2
  319.7 1.0 copy-start.3
  320.7 1.0 copy-start.4
  321.7 0.8 copy-start.5
  322.5 0.8 copy-start.6
where the time goes:
time: 329 us
  Pallas kernels  312 us (95%)
  local copies, waits for them, and re-layouts  12 us (4%)
  other arithmetic  4.12 us (1%)
    pallas_call x1, Pallas kernels, per_device(): pl.pallas_call(functools.partial(mega_kernel, z, tree), out_shape=jax.tre...  306 us
    unnamed x14, local copies, waits for them, and re-layouts  7.48 us

commit v1 on v0

--- a/solution.py
+++ b/solution.py
@@ -17,7 +17,7 @@
 DP, CHAN = "dp", "chan"
 REDUCE, SPLIT, SQUEEZE, EXCITE, EXPAND, SHORTCUT = range(6)
 MATRIX, MID_VECTOR, PAIR_VECTOR, ATT_VECTOR, OUT_VECTOR = range(5)
-SYNC_ROWS = (24, 8, 8, 16, 8, 8, 8, 16, 16, 8, 8, 8, 24, 8, 8, 8)
+SYNC_ROWS = (8, 8, 8, 32, 8, 8, 8, 16, 16, 8, 8, 8, 24, 8, 8, 8)
 
 NT = (((1,), (1,)), ((), ()))
 NN = (((1,), (0,)), ((), ()))
@@ -68,6 +68,8 @@
 class Sizes:
     def __init__(self, mesh, images, reduce_w, expand_w, squeeze_w):
         self.nd, self.nc = mesh.shape[DP], mesh.shape[CHAN]
+        self.near = min(self.nd, 8)
+        self.far = self.nd // self.near
         self.b = images.shape[0] // self.nc
         self.si = images.shape[1]
         self.so = self.si // 2
@@ -103,14 +105,15 @@
             for key in members:
                 self.lay[key] = (group, at)
                 at += self.piece_rows[key]
-            self.rows[group] = -(-at // (16 * self.nd)) * 16 * self.nd
+            self.rows[group] = -(-at // (16 * self.near)) * 16 * self.near
 
 
 GROUPS = {
-    0: ((2, EXPAND), (2, EXCITE), (2, SQUEEZE), (2, SPLIT), (2, REDUCE)),
-    1: ((1, EXPAND), (1, EXCITE), (1, SHORTCUT)),
-    2: ((1, SPLIT), (1, SQUEEZE)),
-    3: ((1, REDUCE),),
+    0: ((2, EXPAND), (2, EXCITE)),
+    1: ((2, SPLIT), (2, SQUEEZE)),
+    2: ((2, REDUCE), (1, EXPAND), (1, EXCITE), (1, SHORTCUT)),
+    3: ((1, SPLIT), (1, SQUEEZE)),
+    4: ((1, REDUCE),),
 }
 VEC_ROWS = {
     1: SimpleNamespace(rg=0, rb=1, sg=2, sb=4, xb=6, eg=8, eb=10, hg=12, hb=14, qg=16, qb=17),
@@ -132,7 +135,7 @@
     return SimpleNamespace(**inner) if all(isinstance(k, str) for k in inner) else inner
 
 
-def scratch_tree(z):
+def scratch_tree(z, vec):
     def f32(*shape):
         return pltpu.VMEM(shape, F32)
 
@@ -148,6 +151,9 @@
         cot=bf16(z.no, z.co),
         wsh=bf16(z.ci, z.co),
         vv=f32(z.nc, NVEC, LANES),
+        vmine=f32(NVEC, LANES),
+        vraw=[f32(*v.shape) for v in vec],
+        vsem=sem(len(vec)),
         mo=f32(z.no, LANES),
         mi=bf16(z.ni, LANES),
         red1=f32(z.mid // LANES, z.b * z.so, 2, z.si, LANES),
@@ -193,13 +199,16 @@
                 pk=bf16(z.nc // 2, 2, rows, LANES),
                 r1=bf16(z.nc // 2, rows, LANES),
                 r2=bf16(rows, LANES),
-                r3=bf16(z.nd, rows // z.nd, LANES),
+                r3=bf16(z.near, rows // z.near, LANES),
+                r4=bf16(z.far, rows // z.near, LANES),
                 q1=sem(2),
                 q2=sem(2),
-                q3s=sem(z.nd),
-                q3r=sem(z.nd),
-                q4s=sem(z.nd),
-                q4r=sem(z.nd),
+                q3s=sem(z.near),
+                q3r=sem(z.near),
+                q4s=sem(z.near),
+                q4r=sem(z.near),
+                q5s=sem(z.far),
+                q5r=sem(z.far),
             )
             for n, rows in z.rows.items()
         },
@@ -216,8 +225,8 @@
         out_got=sem(1 + QUARTERS, z.nc),
         s0s=sem(1),
         s0r=sem(2),
-        s1s=sem(ns),
-        s1r=sem(2, ns),
+        s1s=sem(1),
+        s1r=sem(2),
     )
 
 
@@ -238,6 +247,10 @@
         return (lax.div(s, nc // 2), lax.rem(s, nc // 2) * 2 + odd)
 
     partner = (d, c + 1 - 2 * odd)
+    far_first = []
+    if ns <= 16:
+        for n in range(ns - 1):
+            far_first.append(place(lax.rem(me + (n + ns // 3) % (ns - 1) + 1, ns)))
 
     barrier = pltpu.get_barrier_semaphore()
     for i in range(1, nc):
@@ -281,6 +294,46 @@
                 ).wait_recv()
                 self.copy(i).wait_send()
 
+    class Relay:
+        def __init__(self, src, dst, send, recv):
+            self.src, self.dst, self.send, self.recv = src, dst, send, recv
+            self.far = chan_at(2)
+
+        def copy(self, n, src, which, to):
+            return pltpu.make_async_remote_copy(
+                src_ref=src, dst_ref=self.dst(which), send_sem=self.send.at[n],
+                recv_sem=self.recv.at[n], device_id=to, device_id_type=MESH,
+            )
+
+        def across(self, which):
+            return self.copy(1, self.src(c), which, (d, self.far))
+
+        def beside(self, which):
+            return self.copy(2, self.src(c), which, partner)
+
+        def onward(self, which):
+            return self.copy(3, self.dst(self.far), which, partner)
+
+        def local(self):
+            return pltpu.make_async_copy(self.src(c), self.dst(c), self.recv.at[0])
+
+        def start(self):
+            self.across(c).start()
+            self.beside(c).start()
+            self.local().start()
+
+        def forward(self):
+            self.across(self.far).wait_recv()
+            self.onward(self.far).start()
+
+        def wait(self):
+            self.local().wait()
+            self.across(c).wait_send()
+            self.beside(c).wait_send()
+            self.onward(self.far).wait_send()
+            self.beside(partner[1]).wait_recv()
+            self.onward(lax.rem(partner[1] + 2, nc)).wait_recv()
+
     gs_sem, gr_sem = r.gather_send, r.gather_recv
     xs_sem, xr_sem = r.image_send, r.image_recv
     os_sem, or_sem = r.out_send, r.out_got
@@ -301,14 +354,14 @@
     ms = z.mids
     sem_rows = iter(range(13))
 
-    def gathered(src, dst):
+    def gathered(src, dst, kind=Relay):
         e = next(sem_rows)
-        return Exchange(src, dst, gs_sem.at[e], gr_sem.at[e])
+        return kind(src, dst, gs_sem.at[e], gr_sem.at[e])
 
     ex = SimpleNamespace(
-        vec=gathered(whole(given.vec), lambda s: r.vv.at[s]),
+        vec=gathered(whole(r.vmine), lambda s: r.vv.at[s], Exchange),
         wsh=gathered(whole(given.wsh), lanes_of(r.wsh, z.cos)),
-        cot=gathered(rows_of(given.cot, no), lanes_of(r.cot, z.cos)),
+        cot=gathered(rows_of(given.cot, no), lanes_of(r.cot, z.cos), Exchange),
         blk={
             k: SimpleNamespace(
                 wrt=gathered(whole(given.blk[k].wrt), rows_of(r.blk[k].wrt, ms)),
@@ -332,17 +385,28 @@
             xs_sem.at[q],
             xr_sem.at[q],
         ))
-    ex.blk[1].wrt.start()
-    ex.vec.start()
+    first_w, second_w = ex.blk[1], ex.blk[2]
+    first_w.wrt.start()
+    raw = [
+        pltpu.make_async_copy(v, to, r.vsem.at[n]) for n, (v, to) in enumerate(zip(given.vec, r.vraw))
+    ]
+    for copy in raw:
+        copy.start()
     ex.x[0].start()
-    ex.wsh.start()
     for q in range(1, nq):
         ex.x[q].start()
-    for k in (1, 2):
-        w = ex.blk[k]
-        for e in ((w.wst, w.sq, w.ext, w.we) if k == 1 else (w.wrt, w.wst, w.sq, w.ext, w.we)):
-            e.start()
-    ex.cot.start()
+    row = 0
+    for copy, v in zip(raw, r.vraw):
+        copy.wait()
+        rows, width = v.shape
+        for k in range(rows):
+            one = v[k : k + 1, :]
+            if width < LANES:
+                one = jnp.concatenate([one, one], axis=1)
+            for t in range(one.shape[1] // LANES):
+                r.vmine[row : row + 1, :] = one[:, t * LANES : (t + 1) * LANES]
+                row += 1
+    ex.vec.start()
 
     ss0, rs0, ss1, rs1 = r.s0s, r.s0r, r.s1s, r.s1r
 
@@ -365,29 +429,29 @@
         pair = sa[...] + sb[...]
         sc[me] = pair
 
-        def send(i, _):
-            j = lax.rem(i + ns // 3, ns - 1) + 1
+        def send(to):
             pltpu.make_async_remote_copy(
-                src_ref=sc.at[me], dst_ref=sc.at[me], send_sem=ss1.at[j],
-                recv_sem=rs1.at[k % 2, me], device_id=place(lax.rem(me + j, ns)),
-                device_id_type=MESH,
+                src_ref=sc.at[me], dst_ref=sc.at[me], send_sem=ss1.at[0],
+                recv_sem=rs1.at[k % 2], device_id=to, device_id_type=MESH,
             ).start()
-            return 0
-
-        lax.fori_loop(0, ns - 1, send, 0)
-
+
+        if ns <= 16:
+            for to in far_first:
+                send(to)
+        else:
+
+            def send_one(j, _):
+                send(place(lax.rem(me + j, ns)))
+                return 0
+
+            lax.fori_loop(1, ns, send_one, 0)
         if meanwhile is not None:
             meanwhile()
-
-        def arrive(j, _):
-            s = lax.rem(me + j, ns)
-            pltpu.make_async_remote_copy(
-                src_ref=sc.at[me], dst_ref=sc.at[s], send_sem=ss1.at[j],
-                recv_sem=rs1.at[k % 2, s], device_id=place(s), device_id_type=MESH,
-            ).wait()
-            return 0
-
-        lax.fori_loop(1, ns, arrive, 0)
+        others = sc.at[pl.ds(0, ns - 1)]
+        pltpu.make_async_remote_copy(
+            src_ref=others, dst_ref=others, send_sem=ss1.at[0], recv_sem=rs1.at[k % 2],
+            device_id=partner, device_id_type=MESH,
+        ).wait()
         if ns <= 16:
             total = sc[0]
             for s in range(1, ns):
@@ -520,7 +584,8 @@
         return red1[t, lead, p, pl.ds(q, so, stride=2), :].reshape(4 * so, LANES)
 
     pool_m = pool_matrix(0)
-    ex.blk[1].wrt.wait()
+    first_w.wrt.forward()
+    first_w.wrt.wait()
     r1, r2 = zero8(mid), zero8(mid)
     for q in range(nq):
         ex.x[q].wait()
@@ -540,30 +605,28 @@
             return s1 + sum8(mv), s2 + sum8(mv * v)
 
         r1, r2 = lax.fori_loop(0, lead, red_sums, (r1, r2))
-        pooled = dot(pool_m, xv).astype(BF16)
-        r.pool[q * pool_rows : (q + 1) * pool_rows, :] = pooled
-    ex.wsh.wait()
-    for n0 in range(0, co, 256):
-        r.short[:, n0 : n0 + 256] = dot(r.pool[...], r.wsh[:, n0 : n0 + 256])
-    h1, h2 = moments(r.short, no, co, 16)
+    first_w.wst.start()
     put(0, 0, fold(r1))
     put(0, mid // LANES, fold(r2))
     at = 2 * mid // LANES
-    put(0, at, h1)
-    put(0, at + co // LANES, h2)
     local_area = areas[0]
     for k in range(1, b):
         local_area = local_area + areas[k]
-    put(0, at + 2 * co // LANES, jnp.full((1, LANES), local_area, F32))
-    allreduce(0, at + 2 * co // LANES + 1)
+    put(0, at, jnp.full((1, LANES), local_area, F32))
+
+    def pooling():
+        for q in range(nq):
+            r.pool[q * pool_rows : (q + 1) * pool_rows, :] = dot(
+                pool_m, r.x[q * part : (q + 1) * part, :]
+            ).astype(BF16)
+
+    allreduce(0, at + 1, pooling)
     ex.vec.wait()
-    count = total(0, at + 2 * co // LANES, LANES)
+    count = total(0, at, LANES)
     inv_out = 1.0 / count
     inv_in = 0.25 * inv_out
     vr1, vr2 = VEC_ROWS[1], VEC_ROWS[2]
     nred1 = norm(0, 0, mid // LANES, mid, inv_in, v_mid(vr1.rg), v_mid(vr1.rb))
-    nshort = norm(0, at, at + co // LANES, co, inv_out, v_co(vr1.hg), v_co(vr1.hb))
-
     lane16 = lax.rem(lax.broadcasted_iota(jnp.int32, (4 * so, mid), 0), so)
     not_first = lane16 > 0
     not_last = lane16 < so - 1
@@ -603,7 +666,10 @@
                         im_put(im1, at, wj, di, dj, 1 if di == 0 else 0)
         return 0
 
+    for e in (first_w.sq, first_w.ext, first_w.we, ex.wsh):
+        e.start()
     lax.fori_loop(0, no // (4 * so), build1, 0)
+    first_w.wst.forward()
     im_zero(im1, 0, False)
 
     def split_weights(k, g):
@@ -617,11 +683,11 @@
             )
         return moments(r.blk[k].sp, no, 2 * mid, 32)
 
-    def attention_forward(k, vr, sync):
+    def attention_forward(k, vr, sync, fills):
         s1, s2 = split_conv(k)
         put(sync, 0, s1)
         put(sync, 4, s2)
-        allreduce(sync, 8)
+        allreduce(sync, 8, fills[0])
         nsplit = norm(sync, 0, 4, 2 * mid, inv_out, v_split(vr.sg), v_split(vr.sb))
         sp, sa, pm = r.blk[k].sp, r.blk[k].sa, r.blk[k].pm
         for img in range(b):
@@ -639,7 +705,7 @@
         put(sync + 1, 0, fold(squeezed))
         put(sync + 1, 1, fold(squeezed * squeezed))
         put(sync + 1, 2, fold(pm[...]))
-        allreduce(sync + 1, 4)
+        allreduce(sync + 1, 4, fills[1])
         inv_images = jnp.full((1, LANES), 1.0 / (b * nc * nd), F32)
         natt = norm(
             sync + 1, 0, 1, att, inv_images, vv[0, vr.qg : vr.qg + 1, :],
@@ -674,11 +740,40 @@
         s1, s2 = moments(r.blk[k].exp, no, co, 16)
         put(sync + 2, 0, s1)
         put(sync + 2, co // LANES, s2)
-        allreduce(sync + 2, 2 * co // LANES)
+        if k == 1:
+            for n, v in enumerate(short_sums):
+                put(sync + 2, (2 + n) * co // LANES, v)
+        allreduce(sync + 2, (4 if k == 1 else 2) * co // LANES, fills[2])
         nexp = norm(sync + 2, 0, co // LANES, co, inv_out, v_co(vr.eg), v_co(vr.eb))
         return SimpleNamespace(nsplit=nsplit, natt=natt, xhat=xhat, pre=pre, excited=excited, nexp=nexp, centred=centred)
 
-    f1 = attention_forward(1, vr1, 1)
+    short_sums = []
+
+    def shortcut_forward():
+        ex.wsh.wait()
+        for n0 in range(0, co, 256):
+            r.short[:, n0 : n0 + 256] = dot(r.pool[...], r.wsh[:, n0 : n0 + 256])
+        short_sums.extend(moments(r.short, no, co, 16))
+
+    def forward_first():
+        for e in (first_w.sq, first_w.ext, first_w.we):
+            e.forward()
+        second_w.wrt.start()
+
+    def between():
+        ex.wsh.forward()
+        second_w.wst.start()
+        shortcut_forward()
+
+    def forward_second():
+        second_w.wrt.forward()
+        for e in (second_w.sq, second_w.ext, second_w.we):
+            e.start()
+
+    f1 = attention_forward(1, vr1, 1, (forward_first, between, forward_second))
+    nshort = norm(
+        3, 2 * co // LANES, 3 * co // LANES, co, inv_out, v_co(vr1.hg), v_co(vr1.hb)
+    )
 
     def summed1(rows):
         return (
@@ -700,7 +795,14 @@
     s1, s2 = moments(r.red2, no, mid, 64)
     put(4, 0, s1)
     put(4, 2, s2)
-    allreduce(4, 4)
+
+    def forward_rest():
+        ex.cot.start()
+        second_w.wst.forward()
+        for e in (second_w.sq, second_w.ext, second_w.we):
+            e.forward()
+
+    allreduce(4, 4, forward_rest)
     nred2 = norm(4, 0, 2, mid, inv_out, v_mid(vr2.rg), v_mid(vr2.rb))
     im2 = r.blk[2].im
 
@@ -721,7 +823,7 @@
     lax.fori_loop(0, no // (4 * so), build2, 0)
     im_zero(im2, 0, False)
     im_zero(im2, 2, True)
-    f2 = attention_forward(2, vr2, 5)
+    f2 = attention_forward(2, vr2, 5, (None, None, None))
 
     ex.cot.wait()
 
@@ -771,9 +873,11 @@
             own = r.group[group]
             self.pk, self.r1, self.r2, self.r3 = own.pk, own.r1, own.r2, own.r3
             self.rows = z.rows[group]
-            self.piece = self.rows // nd
+            self.piece = self.rows // z.near
+            self.r4 = own.r4
+            self.near, self.mine = lax.rem(d, z.near), lax.div(d, z.near)
             self.res = made.res[group]
-            self.sems = [own.q1, own.q2, own.q3s, own.q3r, own.q4s, own.q4r]
+            self.sems = [own.q1, own.q2, own.q3s, own.q3r, own.q4s, own.q4r, own.q5s, own.q5r]
             self.across = lax.div(c, 2)
 
         def piece_at(self, n):
@@ -792,24 +896,53 @@
                 device_id=(d, chan_at(2)), device_id_type=MESH,
             )
 
+        def at_near(self, n):
+            return (self.mine * z.near + n, c)
+
         def copy3(self, to, src):
             return pltpu.make_async_remote_copy(
                 src_ref=self.pk.at[self.across, odd, self.piece_at(to), :],
                 dst_ref=self.r3.at[src], send_sem=self.sems[2].at[to],
-                recv_sem=self.sems[3].at[src], device_id=(to, c), device_id_type=MESH,
+                recv_sem=self.sems[3].at[src], device_id=self.at_near(to), device_id_type=MESH,
             )
 
         def copy4(self, to, src):
             return pltpu.make_async_remote_copy(
-                src_ref=self.r3.at[d], dst_ref=self.res.at[self.piece_at(src), :],
+                src_ref=self.r3.at[self.near], dst_ref=self.res.at[self.piece_at(src), :],
                 send_sem=self.sems[4].at[to], recv_sem=self.sems[5].at[src],
-                device_id=(to, c), device_id_type=MESH,
+                device_id=self.at_near(to), device_id_type=MESH,
+            )
+
+        def copy5(self, to, src):
+            return pltpu.make_async_remote_copy(
+                src_ref=self.r4.at[self.mine], dst_ref=self.r4.at[src],
+                send_sem=self.sems[6].at[to], recv_sem=self.sems[7].at[src],
+                device_id=(to * z.near + self.near, c), device_id_type=MESH,
             )
 
         def local4(self):
             return pltpu.make_async_copy(
-                self.r3.at[d], self.res.at[self.piece_at(d), :], self.sems[5].at[d]
+                self.r3.at[self.near], self.res.at[self.piece_at(self.near), :],
+                self.sems[5].at[self.near],
             )
+
+        def others(self, body, me, n):
+            def step(j, _):
+                body(lax.rem(me + j, n), lax.rem(me - j + n, n))
+                return 0
+
+            lax.fori_loop(1, n, step, 0)
+
+        def total(self, slots, n, to):
+            def body(at, _):
+                rows = pl.ds(at, 16)
+                t = slots[0, rows, :].astype(F32)
+                for k in range(1, n):
+                    t = t + slots[k, rows, :].astype(F32)
+                to[rows, :] = t.astype(BF16)
+                return 0
+
+            loop(self.piece, 16, body, 0)
 
         def add(self, which, other):
             def body(at, _):
@@ -834,59 +967,41 @@
         def step3(self):
             self.copy2().wait_recv()
             self.add(self.across, lambda rows: self.r2[rows, :])
-
-            def send(j, _):
-                self.copy3(lax.rem(d + j, nd), d).start()
-                return 0
-
-            lax.fori_loop(1, nd, send, 0)
+            self.others(lambda to, _: self.copy3(to, self.near).start(), self.near, z.near)
             self.copy2().wait_send()
 
         def step4(self):
-            self.r3[d] = self.pk[self.across, odd, self.piece_at(d), :]
-
-            def arrive(j, _):
-                to, src = lax.rem(d + j, nd), lax.rem(d - j + nd, nd)
-                self.copy3(to, d).wait_send()
+            self.r3[self.near] = self.pk[self.across, odd, self.piece_at(self.near), :]
+
+            def arrive(to, src):
+                self.copy3(to, self.near).wait_send()
                 self.copy3(src, src).wait_recv()
-                return 0
-
-            lax.fori_loop(1, nd, arrive, 0)
-
-            def body(at, _):
-                rows = pl.ds(at, 16)
-
-                def term(n, t):
-                    return t + self.r3[n, rows, :].astype(F32)
-
-                t = self.r3[0, rows, :].astype(F32)
-                if nd <= 8:
-                    for n in range(1, nd):
-                        t = term(n, t)
-                else:
-                    t = lax.fori_loop(1, nd, term, t)
-                self.r3[d, rows, :] = t.astype(BF16)
-                return 0
-
-            loop(self.piece, 16, body, 0)
+
+            self.others(arrive, self.near, z.near)
+            mine = self.r3.at[self.near]
+            if z.far == 1:
+                self.total(self.r3, z.near, mine)
+            else:
+                self.total(self.r3, z.near, self.r4.at[self.mine])
+                self.others(lambda to, _: self.copy5(to, self.mine).start(), self.mine, z.far)
+
+                def arrive_far(to, src):
+                    self.copy5(to, self.mine).wait_send()
+                    self.copy5(src, src).wait_recv()
+
+                self.others(arrive_far, self.mine, z.far)
+                self.total(self.r4, z.far, mine)
             self.local4().start()
-
-            def send(j, _):
-                self.copy4(lax.rem(d + j, nd), d).start()
-                return 0
-
-            lax.fori_loop(1, nd, send, 0)
+            self.others(lambda to, _: self.copy4(to, self.near).start(), self.near, z.near)
 
         def finish(self):
             self.local4().wait()
 
-            def arrive(j, _):
-                to, src = lax.rem(d + j, nd), lax.rem(d - j + nd, nd)
-                self.copy4(to, d).wait_send()
+            def arrive(to, src):
+                self.copy4(to, self.near).wait_send()
                 self.copy4(src, src).wait_recv()
-                return 0
-
-            lax.fori_loop(1, nd, arrive, 0)
+
+            self.others(arrive, self.near, z.near)
 
     sums_of = {group: Reduction(group) for group in GROUPS}
 
@@ -947,8 +1062,12 @@
                 for s in range(nc):
                     share = slice(s * z.cos, (s + 1) * z.cos)
                     pack_lanes(k, SHORTCUT, s, dot(r.sgt[...], r.shg[:, share]))
-                sums_of[1].step1()
+                sums_of[2].step1()
+                sums_of[1].step3()
                 r.pg[...] = dot(r.shg[...], r.wsh[...], NT).astype(BF16)
+
+            else:
+                sums_of[0].step1()
 
         allreduce(sync + 1, 6, matrices)
         inv_images = 1.0 / (b * nc * nd)
@@ -957,9 +1076,7 @@
         keep(srow.qg, sux)
         keep(srow.xb, total(sync + 1, 2, 2 * mid))
         sb = natt.gs * (au - su * inv_images - f.xhat * (sux * inv_images)) * live8
-        if first:
-            sums_of[0].step3()
-            sums_of[1].step2()
+        sums_of[2 if first else 0].step2()
         r.mgr[...] = dot_exact(sb, r.blk[k].sq[...], NT) * tiled(inv_area, mid)
         sp = r.blk[k].sp
         carry = (zero8(2 * mid), zero8(2 * mid))
@@ -981,6 +1098,8 @@
         put(sync + 2, 4, fold(carry[1]))
 
         def squeeze_matrix():
+            if first:
+                sums_of[1].step4()
             pack_rows(k, SQUEEZE, 0, dot_exact(f.centred, sb, TN))
 
         allreduce(sync + 2, 8, squeeze_matrix)
@@ -1064,7 +1183,13 @@
         sums.append(carry)
     put(11, 0, jnp.concatenate([fold(s[0]) for s in sums], axis=1))
     put(11, 2, jnp.concatenate([fold(s[1]) for s in sums], axis=1))
-    allreduce(11, 4, lambda: split_matrix(2))
+    def split_matrix2():
+        split_matrix(2)
+        sums_of[1].step1()
+        sums_of[0].step3()
+
+    allreduce(11, 4, split_matrix2)
+    sums_of[1].step2()
     su, sux, ca, cb = norm_grad(11, 0, 2, mid, inv_out, nred2)
     keep(STO_ROWS[2].rb, su)
     keep(STO_ROWS[2].rg, sux)
@@ -1102,10 +1227,9 @@
         r.rgt[:, :no] = jnp.transpose(r.rg1[:no, :])
         for n0 in range(0, co, 256):
             pack_rows(2, REDUCE, n0 // LANES, dot(r.rgt[:, :no], r.h[:, n0 : n0 + 256]))
-        sums_of[0].step1()
+        sums_of[0].step4()
 
     allreduce(12, 3 * co // LANES, reduce_matrix2)
-    sums_of[0].step2()
 
     attention_backward(1, f1, 12)
     sums = []
@@ -1141,11 +1265,9 @@
 
     def split_matrix1():
         split_matrix(1)
-        sums_of[2].step1()
+        sums_of[3].step1()
 
     allreduce(15, 4, split_matrix1)
-    sums_of[0].step4()
-    sums_of[2].step2()
     su, sux, ca, cb = norm_grad(15, 0, 2, mid, inv_in, nred1)
     keep(STO_ROWS[1].rb, su)
     keep(STO_ROWS[1].rg, sux)
@@ -1157,26 +1279,24 @@
         r.rg1[rows, :] = (nred1.gs * u - m * (ca + cb * v)).astype(BF16)
         return 0
 
-    lax.fori_loop(0, b * so, reduce_grad1, 0)
-    r.rgt[...] = jnp.transpose(r.rg1[...])
-    for n0 in range(0, ci, 256):
-        pack_rows(1, REDUCE, n0 // LANES, dot(r.rgt[...], r.x[:, n0 : n0 + 256]))
-    sums_of[3].step1()
-    sums_of[1].step3()
     spread = pool_matrix(1)
+    grads = (r.h, r.eg)
     last = []
     for q in range(nq):
         rows = slice(q * part, (q + 1) * part)
+        lead = part // (2 * si)
+        lax.fori_loop(q * lead, (q + 1) * lead, reduce_grad1, 0)
         m = tiled(r.mi[rows, :].astype(F32), 256)
         for n0 in range(0, ci, 256):
             cols = slice(n0, n0 + 256)
             v = dot(r.rg1[rows, :], r.blk[1].wrt[:, cols]) + dot(
                 spread, r.pg[q * pool_rows : (q + 1) * pool_rows, cols]
             )
-            r.x[rows, cols] = (v * m).astype(BF16)
+            at = (q % 2) * ci + n0
+            grads[q // 2][:, at : at + 256] = (v * m).astype(BF16)
         e = Exchange(
-            lambda s, q=q: r.x.at[
-                pl.ds(q * part, part), pl.ds(pl.multiple_of(s * z.cis, LANES), z.cis)
+            lambda s, q=q: grads[q // 2].at[
+                :, pl.ds(pl.multiple_of((q % 2) * ci + s * z.cis, LANES), z.cis)
             ],
             lambda s, q=q: made.gx.at[
                 pl.ds(pl.multiple_of(s * ni + q * part, part), part), :
@@ -1186,16 +1306,23 @@
         )
         e.start()
         last.append(e)
-    sums_of[3].step2()
-    sums_of[2].step3()
-    sums_of[1].step4()
+        if q == 0:
+            sums_of[3].step2()
+            sums_of[2].step3()
+    r.rgt[...] = jnp.transpose(r.rg1[...])
+    for n0 in range(0, ci, 256):
+        pack_rows(1, REDUCE, n0 // LANES, dot(r.rgt[...], r.x[:, n0 : n0 + 256]))
+    sums_of[4].step1()
+    sums_of[2].step4()
+    sums_of[4].step2()
     sums_of[3].step3()
-    sums_of[2].step4()
+    sums_of[4].step3()
     sums_of[3].step4()
+    sums_of[4].step4()
     out_ex.wait()
     for e in last:
         e.wait()
-    for sums in (sums_of[0], sums_of[1], sums_of[2], sums_of[3]):
+    for sums in sums_of.values():
         sums.finish()
 
 
@@ -1220,12 +1347,9 @@
     z = Sizes(mesh, images, first.reduce, first.expand, first.squeeze)
 
     def vectors(w):
-        parts = [
-            doubled(w.reducegain[None]), doubled(w.reducebias[None]),
-            doubled(w.splitgain), doubled(w.splitbias), doubled(w.excitebias),
-        ]
-        parts += [v.reshape(-1, LANES) for v in (w.expandgain, w.expandbias) + w.extra[1:]]
-        return parts + [w.squeezegain.reshape(-1, LANES), w.squeezebias.reshape(-1, LANES)]
+        parts = (w.reducegain, w.reducebias, w.splitgain, w.splitbias, w.excitebias)
+        parts += (w.expandgain, w.expandbias) + w.extra[1:] + (w.squeezegain, w.squeezebias)
+        return [v if v.ndim == 2 else v.reshape(1, -1) for v in parts]
 
     def block(w):
         return dict(
@@ -1240,7 +1364,7 @@
         images=images.reshape(-1, z.cis),
         cot=cotangent.reshape(-1, z.cos),
         groups=groups,
-        vec=jnp.concatenate(vectors(first) + vectors(second), axis=0),
+        vec=vectors(first) + vectors(second),
         wsh=first.extra[0],
         blk={1: block(first), 2: block(second)},
     )
@@ -1254,7 +1378,7 @@
     )
     out_specs = jax.tree.map(lambda v: pl.BlockSpec(memory_space=pl.ANY), outs)
     out_specs.update(sto=pl.BlockSpec(memory_space=pltpu.VMEM))
-    scratch = scratch_tree(z)
+    scratch = scratch_tree(z, vectors(first) + vectors(second))
     tree = jax.tree.structure((inputs, outs, scratch))
     results = pl.pallas_call(
         functools.partial(mega_kernel, z, tree),
@@ -1263,7 +1387,7 @@
         out_specs=jax.tree.leaves(out_specs),
         scratch_shapes=jax.tree.leaves(scratch),
         compiler_params=pltpu.CompilerParams(
-            collective_id=0, has_side_effects=True, vmem_limit_bytes=62 << 20
+            collective_id=0, has_side_effects=True, vmem_limit_bytes=63 << 20
         ),
         name="two_blocks",
     )(*jax.tree.leaves(inputs))
@@ -1348,7 +1472,7 @@
         out_shape=outs,
         in_specs=jax.tree.leaves(in_specs),
         out_specs=[slab(v) for v in images] + [whole(s) for s in shapes],
-        compiler_params=pltpu.CompilerParams(vmem_limit_bytes=40 << 20),
+        compiler_params=pltpu.CompilerParams(vmem_limit_bytes=62 << 20),
         name="unpack",
     )(*jax.tree.leaves(results))
     final = [

time: 329 us -> 254 us (0.77)
  Pallas kernels: 312 us -> 253 us
  local copies, waits for them, and re-layouts: 12 us -> 0 us
  other arithmetic: 4.12 us -> 0 us
    pallas_call x1, Pallas kernels: 306 us -> 245 us  [per_device(): pl.pallas_call(functools.partial(mega_kernel, z, tree), out_shape=jax.tre...]
    unnamed x14 -> x0, local copies, waits for them, and re-layouts: 7.48 us -> none
    concatenate x1 -> x0, local copies, waits for them, and re-layouts: 4.52 us -> none  [per_device(): jnp.concatenate(vectors(first) + vectors(second), axis=0)]
    concatenate x5 -> x0, other arithmetic: 4.12 us -> none  [doubled(): return jnp.concatenate([v, v], axis=-1).reshape(-1, LANES)]
    pallas_call x1, Pallas kernels: 5.18 us -> 8.49 us  [unpack(): pl.pallas_call(functools.partial(unpack_kernel, z, plan, jax.tree.structu...]
where the time goes in v1:
time: 254 us
  Pallas kernels  253 us (100%)
    pallas_call x1, Pallas kernels, per_device(): pl.pallas_call(functools.partial(mega_kernel, z, tree), out_shape=jax.tre...  245 us
    pallas_call x1, Pallas kernels, unpack(): pl.pallas_call(functools.partial(unpack_kernel, z, plan, jax.tree.structu...  8.49 us

profile of v1, /device:TPU:0, one launch (start us, length us, event | category | flops | bytes accessed | tf_op | source)
XLA Modules:
  0.0 254.2 jit_solution(9467088449342375781)
XLA Ops:
  0.7 244.8 %two_blocks.1 = (bf16[8192,128]{1,0:T(8,128)(2,1)}, bf16[2048,256]{1,0:T(8,128)(2,1)}, bf16[640,128]{1,0:T(8,128)(2,1)}, bf16[1280,128]{1,0:T(8,128)(2,1)}, bf16...) custom-call(bf16[2,64,128]{2,1,0:T(8,128)(2,1)} %bitcast.62, ...), custom_call_target="tpu_custom_call" | custom-call | tf_op jit(solution)/shard_map/two_blocks/pallas_call | solution.py:1383
  245.5 8.5 %unpack.1 = (f32[2048,256]{1,0:T(8,128)}, f32[8192,128]{1,0:T(8,128)}, f32[64,512]{1,0:T(8,128)}, f32[1,64]{1,0:T(1,128)}, f32[1,64]{1,0:T(1,128)}, /*index=5*/f...) custom-call(bf16[8192,128]{1,0:T(8,128)(2,1)} %get-tuple-element.74., ...), custom_call_target="tpu_custom_call" | custom-call | tf_op jit(solution)/shard_map/unpack/pallas_call | solution.py:1469

commit v2 on v1

--- a/solution.py
+++ b/solution.py
@@ -111,9 +111,10 @@
 GROUPS = {
     0: ((2, EXPAND), (2, EXCITE)),
     1: ((2, SPLIT), (2, SQUEEZE)),
-    2: ((2, REDUCE), (1, EXPAND), (1, EXCITE), (1, SHORTCUT)),
+    2: ((1, EXPAND), (1, EXCITE), (1, SHORTCUT)),
     3: ((1, SPLIT), (1, SQUEEZE)),
     4: ((1, REDUCE),),
+    5: ((2, REDUCE),),
 }
 VEC_ROWS = {
     1: SimpleNamespace(rg=0, rb=1, sg=2, sb=4, xb=6, eg=8, eb=10, hg=12, hb=14, qg=16, qb=17),
@@ -126,6 +127,7 @@
 }
 NSTO = 80
 QUARTERS = 4
+OUT_PARTS = 4
 
 
 def space(tree):
@@ -209,6 +211,8 @@
                 q4r=sem(z.near),
                 q5s=sem(z.far),
                 q5r=sem(z.far),
+                ry=bf16(rows // 2 if n == 2 else 16, LANES),
+                q6=sem(4),
             )
             for n, rows in z.rows.items()
         },
@@ -221,8 +225,8 @@
         gather_recv=sem(13, z.nc),
         image_send=sem(QUARTERS, z.nc),
         image_recv=sem(QUARTERS, z.nc),
-        out_send=sem(1 + QUARTERS, z.nc),
-        out_got=sem(1 + QUARTERS, z.nc),
+        out_send=sem(OUT_PARTS + QUARTERS, z.nc),
+        out_got=sem(OUT_PARTS + QUARTERS, z.nc),
         s0s=sem(1),
         s0r=sem(2),
         s1s=sem(1),
@@ -840,16 +844,24 @@
         return su + sum8(u), sv + sum8(u * v)
 
     su, sv = loop(no, 16, finish, (zero8(co), zero8(co)))
-    out_ex = Exchange(
-        lambda s: r.cot.at[:, pl.ds(pl.multiple_of(s * z.cos, LANES), z.cos)],
-        lambda s: made.out.at[pl.ds(pl.multiple_of(s * no, no), no), :],
-        os_sem.at[0],
-        or_sem.at[0],
-    )
-    out_ex.start()
+    out_part = no // OUT_PARTS
+    out_ex = [
+        Exchange(
+            lambda s, n=n: r.cot.at[
+                pl.ds(n * out_part, out_part), pl.ds(pl.multiple_of(s * z.cos, LANES), z.cos)
+            ],
+            lambda s, n=n: made.out.at[
+                pl.ds(pl.multiple_of(s * no + n * out_part, out_part), out_part), :
+            ],
+            os_sem.at[n],
+            or_sem.at[n],
+        )
+        for n in range(OUT_PARTS)
+    ]
     put(8, 0, fold(su))
     put(8, co // LANES, fold(sv))
     allreduce(8, 2 * co // LANES)
+    out_ex[0].start()
 
     def pack_rows(k, name, skip, v):
         group, at = z.lay[(k, name)]
@@ -957,20 +969,22 @@
         def step1(self):
             self.copy1().start()
 
+        def ready2(self):
+            self.copy1().wait()
+            for which in (1 - self.across, self.across):
+                self.add(which, lambda rows, which=which: self.r1[which, rows, :])
+
         def step2(self):
-            self.copy1().wait()
-            away = 1 - self.across
-            self.add(away, lambda rows: self.r1[away, rows, :])
             self.copy2().start()
-            self.add(self.across, lambda rows: self.r1[self.across, rows, :])
+
+        def ready3(self):
+            self.copy2().wait()
+            self.add(self.across, lambda rows: self.r2[rows, :])
 
         def step3(self):
-            self.copy2().wait_recv()
-            self.add(self.across, lambda rows: self.r2[rows, :])
             self.others(lambda to, _: self.copy3(to, self.near).start(), self.near, z.near)
-            self.copy2().wait_send()
-
-        def step4(self):
+
+        def ready4(self):
             self.r3[self.near] = self.pk[self.across, odd, self.piece_at(self.near), :]
 
             def arrive(to, src):
@@ -991,6 +1005,8 @@
 
                 self.others(arrive_far, self.mine, z.far)
                 self.total(self.r4, z.far, mine)
+
+        def step4(self):
             self.local4().start()
             self.others(lambda to, _: self.copy4(to, self.near).start(), self.near, z.near)
 
@@ -1003,7 +1019,121 @@
 
             self.others(arrive, self.near, z.near)
 
-    sums_of = {group: Reduction(group) for group in GROUPS}
+    class SplitReduction(Reduction):
+        def __init__(self, group):
+            super().__init__(group)
+            self.ry, self.q6 = r.group[group].ry, r.group[group].q6
+            self.half = self.rows // 2
+            self.par, self.far_at = lax.rem(self.near, 2), lax.div(self.near, 2)
+            self.quad = z.near // 2
+            self.mate = self.at_near(self.near + 1 - 2 * self.par)
+
+        def half_at(self, par):
+            return pl.ds(pl.multiple_of(par * self.half, 16), self.half)
+
+        def piece_at(self, n):
+            at = lax.rem(n, 2) * self.half + lax.div(n, 2) * self.piece
+            return pl.ds(pl.multiple_of(at, 16), self.piece)
+
+        def copy_half(self):
+            return pltpu.make_async_remote_copy(
+                src_ref=self.pk.at[self.across, odd, self.half_at(1 - self.par), :],
+                dst_ref=self.ry, send_sem=self.q6.at[0], recv_sem=self.q6.at[1],
+                device_id=self.mate, device_id_type=MESH,
+            )
+
+        def copy_back(self, par):
+            rows = self.half_at(par)
+            return pltpu.make_async_remote_copy(
+                src_ref=self.res.at[rows, :], dst_ref=self.res.at[rows, :],
+                send_sem=self.q6.at[2], recv_sem=self.q6.at[3],
+                device_id=self.mate, device_id_type=MESH,
+            )
+
+        def slot3(self, to, src):
+            n = 2 * to + self.par
+            return pltpu.make_async_remote_copy(
+                src_ref=self.pk.at[self.across, odd, self.piece_at(n), :],
+                dst_ref=self.r3.at[src], send_sem=self.sems[2].at[to],
+                recv_sem=self.sems[3].at[src], device_id=self.at_near(n), device_id_type=MESH,
+            )
+
+        def slot4(self, to, src):
+            return pltpu.make_async_remote_copy(
+                src_ref=self.r3.at[self.far_at],
+                dst_ref=self.res.at[self.piece_at(2 * src + self.par), :],
+                send_sem=self.sems[4].at[to], recv_sem=self.sems[5].at[src],
+                device_id=self.at_near(2 * to + self.par), device_id_type=MESH,
+            )
+
+        def local5(self):
+            return pltpu.make_async_copy(
+                self.r3.at[self.far_at], self.res.at[self.piece_at(self.near), :],
+                self.sems[5].at[self.far_at],
+            )
+
+        def step3(self):
+            self.copy_half().start()
+
+        def ready4(self):
+            self.copy_half().wait()
+
+            def body(at, _):
+                rows = pl.ds(pl.multiple_of(self.par * self.half + at, 16), 16)
+                self.pk[self.across, odd, rows, :] = (
+                    self.pk[self.across, odd, rows, :].astype(F32)
+                    + self.ry[pl.ds(at, 16), :].astype(F32)
+                ).astype(BF16)
+                return 0
+
+            loop(self.half, 16, body, 0)
+
+        def step4(self):
+            self.others(lambda to, _: self.slot3(to, self.far_at).start(), self.far_at, self.quad)
+
+        def ready5(self):
+            self.r3[self.far_at] = self.pk[self.across, odd, self.piece_at(self.near), :]
+
+            def arrive(to, src):
+                self.slot3(to, self.far_at).wait_send()
+                self.slot3(src, src).wait_recv()
+
+            self.others(arrive, self.far_at, self.quad)
+            mine = self.r3.at[self.far_at]
+            if z.far == 1:
+                self.total(self.r3, self.quad, mine)
+            else:
+                self.total(self.r3, self.quad, self.r4.at[self.mine])
+                self.others(lambda to, _: self.copy5(to, self.mine).start(), self.mine, z.far)
+
+                def arrive_far(to, src):
+                    self.copy5(to, self.mine).wait_send()
+                    self.copy5(src, src).wait_recv()
+
+                self.others(arrive_far, self.mine, z.far)
+                self.total(self.r4, z.far, mine)
+
+        def step5(self):
+            self.local5().start()
+            self.others(lambda to, _: self.slot4(to, self.far_at).start(), self.far_at, self.quad)
+
+        def ready6(self):
+            self.local5().wait()
+
+            def arrive(to, src):
+                self.slot4(to, self.far_at).wait_send()
+                self.slot4(src, src).wait_recv()
+
+            self.others(arrive, self.far_at, self.quad)
+
+        def step6(self):
+            self.copy_back(self.par).start()
+
+        def finish(self):
+            self.copy_back(self.par).wait_send()
+            self.copy_back(1 - self.par).wait_recv()
+
+    sums_of = {group: (SplitReduction if group == 2 else Reduction)(group) for group in GROUPS}
 
     def attention_backward(k, f, sync):
         srow = STO_ROWS[k]
@@ -1063,7 +1193,8 @@
                     share = slice(s * z.cos, (s + 1) * z.cos)
                     pack_lanes(k, SHORTCUT, s, dot(r.sgt[...], r.shg[:, share]))
                 sums_of[2].step1()
-                sums_of[1].step3()
+                sums_of[5].ready2()
+                sums_of[1].ready3()
                 r.pg[...] = dot(r.shg[...], r.wsh[...], NT).astype(BF16)
 
             else:
@@ -1076,7 +1207,12 @@
         keep(srow.qg, sux)
         keep(srow.xb, total(sync + 1, 2, 2 * mid))
         sb = natt.gs * (au - su * inv_images - f.xhat * (sux * inv_images)) * live8
-        sums_of[2 if first else 0].step2()
+        if first:
+            sums_of[1].step3()
+            sums_of[2].ready2()
+            sums_of[2].step2()
+        else:
+            out_ex[1].start()
         r.mgr[...] = dot_exact(sb, r.blk[k].sq[...], NT) * tiled(inv_area, mid)
         sp = r.blk[k].sp
         carry = (zero8(2 * mid), zero8(2 * mid))
@@ -1098,11 +1234,19 @@
         put(sync + 2, 4, fold(carry[1]))
 
         def squeeze_matrix():
+            pack_rows(k, SQUEEZE, 0, dot_exact(f.centred, sb, TN))
             if first:
-                sums_of[1].step4()
-            pack_rows(k, SQUEEZE, 0, dot_exact(f.centred, sb, TN))
+                sums_of[1].ready4()
+            else:
+                sums_of[0].ready2()
 
         allreduce(sync + 2, 8, squeeze_matrix)
+        if first:
+            sums_of[1].step4()
+            sums_of[5].step2()
+        else:
+            sums_of[0].step2()
+            out_ex[2].start()
         su, sux, ca, cb = norm_grad(sync + 2, 0, 4, 2 * mid, inv_out, nsplit)
         keep(srow.sb, su)
         keep(srow.sg, sux)
@@ -1186,10 +1330,11 @@
     def split_matrix2():
         split_matrix(2)
         sums_of[1].step1()
-        sums_of[0].step3()
+        sums_of[0].ready3()
 
     allreduce(11, 4, split_matrix2)
-    sums_of[1].step2()
+    sums_of[0].step3()
+    out_ex[3].start()
     su, sux, ca, cb = norm_grad(11, 0, 2, mid, inv_out, nred2)
     keep(STO_ROWS[2].rb, su)
     keep(STO_ROWS[2].rg, sux)
@@ -1227,9 +1372,13 @@
         r.rgt[:, :no] = jnp.transpose(r.rg1[:no, :])
         for n0 in range(0, co, 256):
             pack_rows(2, REDUCE, n0 // LANES, dot(r.rgt[:, :no], r.h[:, n0 : n0 + 256]))
-        sums_of[0].step4()
+        sums_of[5].step1()
+        sums_of[1].ready2()
+        sums_of[0].ready4()
 
     allreduce(12, 3 * co // LANES, reduce_matrix2)
+    sums_of[1].step2()
+    sums_of[0].step4()
 
     attention_backward(1, f1, 12)
     sums = []
@@ -1266,8 +1415,13 @@
     def split_matrix1():
         split_matrix(1)
         sums_of[3].step1()
+        sums_of[2].ready3()
+        sums_of[2].step3()
+        sums_of[3].ready2()
+        sums_of[5].ready3()
 
     allreduce(15, 4, split_matrix1)
+    sums_of[5].step3()
     su, sux, ca, cb = norm_grad(15, 0, 2, mid, inv_in, nred1)
     keep(STO_ROWS[1].rb, su)
     keep(STO_ROWS[1].rg, sux)
@@ -1282,10 +1436,9 @@
     spread = pool_matrix(1)
     grads = (r.h, r.eg)
     last = []
-    for q in range(nq):
+
+    def send_quarter(q):
         rows = slice(q * part, (q + 1) * part)
-        lead = part // (2 * si)
-        lax.fori_loop(q * lead, (q + 1) * lead, reduce_grad1, 0)
         m = tiled(r.mi[rows, :].astype(F32), 256)
         for n0 in range(0, ci, 256):
             cols = slice(n0, n0 + 256)
@@ -1301,26 +1454,43 @@
             lambda s, q=q: made.gx.at[
                 pl.ds(pl.multiple_of(s * ni + q * part, part), part), :
             ],
-            os_sem.at[1 + q],
-            or_sem.at[1 + q],
+            os_sem.at[OUT_PARTS + q],
+            or_sem.at[OUT_PARTS + q],
         )
         e.start()
         last.append(e)
-        if q == 0:
-            sums_of[3].step2()
-            sums_of[2].step3()
+
+    lead = part // (2 * si)
+    lax.fori_loop(0, lead, reduce_grad1, 0)
+    send_quarter(0)
+    sums_of[3].step2()
+    sums_of[2].ready4()
+    sums_of[2].step4()
+    lax.fori_loop(lead, nq * lead, reduce_grad1, 0)
     r.rgt[...] = jnp.transpose(r.rg1[...])
     for n0 in range(0, ci, 256):
         pack_rows(1, REDUCE, n0 // LANES, dot(r.rgt[...], r.x[:, n0 : n0 + 256]))
     sums_of[4].step1()
-    sums_of[2].step4()
+    send_quarter(1)
+    sums_of[4].ready2()
     sums_of[4].step2()
+    for q in range(2, nq):
+        send_quarter(q)
+    sums_of[5].ready4()
+    sums_of[5].step4()
+    sums_of[2].ready5()
+    sums_of[2].step5()
+    sums_of[3].ready3()
     sums_of[3].step3()
+    sums_of[4].ready3()
     sums_of[4].step3()
+    sums_of[2].ready6()
+    sums_of[2].step6()
+    sums_of[3].ready4()
     sums_of[3].step4()
+    sums_of[4].ready4()
     sums_of[4].step4()
-    out_ex.wait()
-    for e in last:
+    for e in out_ex + last:
         e.wait()
     for sums in sums_of.values():
         sums.finish()
@@ -1458,7 +1628,7 @@
         return (None, (1, z.mids), (2, z.mids), (1, z.att), (1, z.cos))[kind]
 
     shapes = [shape_of(*entry) for entry in plan]
-    steps = 8
+    steps = 4
     whole = lambda shape: pl.BlockSpec(shape, lambda i: (0, 0))
     slab = lambda v: pl.BlockSpec((v.shape[0] // steps, v.shape[1]), lambda i: (i, 0))
     in_specs = {n: slab(v) if n in ("out", "gx") else jax.tree.map(lambda a: whole(a.shape), v)

time: 254 us -> 229 us (0.902)
  Pallas kernels: 253 us -> 228 us
    pallas_call x1, Pallas kernels: 245 us -> 221 us  [per_device(): pl.pallas_call(functools.partial(mega_kernel, z, tree), out_shape=jax.tre...]
where the time goes in v2:
time: 229 us
  Pallas kernels  228 us (100%)
    pallas_call x1, Pallas kernels, per_device(): pl.pallas_call(functools.partial(mega_kernel, z, tree), out_shape=jax.tre...  221 us
    pallas_call x1, Pallas kernels, unpack(): pl.pallas_call(functools.partial(unpack_kernel, z, plan, jax.tree.structu...  6.71 us

profile of v2, /device:TPU:0, one launch (start us, length us, event | category | flops | bytes accessed | tf_op | source)
XLA Modules:
  0.0 229.0 jit_solution(6597735751414904555)
XLA Ops:
  0.7 221.4 %two_blocks.1 = (bf16[8192,128]{1,0:T(8,128)(2,1)}, bf16[2048,256]{1,0:T(8,128)(2,1)}, bf16[640,128]{1,0:T(8,128)(2,1)}, bf16[1280,128]{1,0:T(8,128)(2,1)}, bf16...) custom-call(bf16[2,64,128]{2,1,0:T(8,128)(2,1)} %bitcast.62, ...), custom_call_target="tpu_custom_call" | custom-call | tf_op jit(solution)/shard_map/two_blocks/pallas_call | solution.py:1553
  222.1 6.7 %unpack.1 = (f32[2048,256]{1,0:T(8,128)}, f32[8192,128]{1,0:T(8,128)}, f32[64,512]{1,0:T(8,128)}, f32[1,64]{1,0:T(1,128)}, f32[1,64]{1,0:T(1,128)}, /*index=5*/f...) custom-call(bf16[8192,128]{1,0:T(8,128)(2,1)} %get-tuple-element.75., ...), custom_call_target="tpu_custom_call" | custom-call | tf_op jit(solution)/shard_map/unpack/pallas_call | solution.py:1639

commit v3 on v2

--- a/solution.py
+++ b/solution.py
@@ -17,7 +17,7 @@
 DP, CHAN = "dp", "chan"
 REDUCE, SPLIT, SQUEEZE, EXCITE, EXPAND, SHORTCUT = range(6)
 MATRIX, MID_VECTOR, PAIR_VECTOR, ATT_VECTOR, OUT_VECTOR = range(5)
-SYNC_ROWS = (8, 8, 8, 32, 8, 8, 8, 16, 16, 8, 8, 8, 24, 8, 8, 8)
+SYNC_ROWS = (8, 8, 8, 32, 8, 8, 8, 16, 16, 16, 8, 24, 16, 8)
 
 NT = (((1,), (1,)), ((), ()))
 NN = (((1,), (0,)), ((), ()))
@@ -63,6 +63,10 @@
     if isinstance(start, int):
         return pl.ds(start, size)
     return pl.ds(pl.multiple_of(start, size), size)
+
+
+def tile_of(rows):
+    return next(t for t in (256, 128, 64, 32, 16) if rows % t == 0)
 
 
 class Sizes:
@@ -116,6 +120,7 @@
     4: ((1, REDUCE),),
     5: ((2, REDUCE),),
 }
+SPLIT_GROUPS = (1, 2, 3, 5)
 VEC_ROWS = {
     1: SimpleNamespace(rg=0, rb=1, sg=2, sb=4, xb=6, eg=8, eb=10, hg=12, hb=14, qg=16, qb=17),
     2: SimpleNamespace(rg=18, rb=19, sg=20, sb=22, xb=24, eg=26, eb=28, qg=30, qb=31),
@@ -127,6 +132,7 @@
 }
 NSTO = 80
 QUARTERS = 4
+KINDS = 9
 OUT_PARTS = 4
 
 
@@ -178,6 +184,8 @@
         rgt=bf16(z.mid, z.ni),
         pg=bf16(z.no, z.ci),
         ags=f32(8, 2 * z.mid),
+        met=f32(z.nc, KINDS * z.b + 6, LANES),
+        all=f32(z.nd, KINDS, 8, LANES),
         mgr=f32(8, z.mid),
         blk={
             k: dict(
@@ -193,6 +201,10 @@
                 exp=f32(z.no, z.co),
                 att=f32(8, 2 * z.mid),
                 pm=f32(8, z.mid),
+                own=f32(KINDS * z.b + 6, LANES),
+                group=f32(KINDS, 8, LANES),
+                ms=sem(3),
+                mr=sem(3),
             )
             for k in (1, 2)
         },
@@ -211,7 +223,7 @@
                 q4r=sem(z.near),
                 q5s=sem(z.far),
                 q5r=sem(z.far),
-                ry=bf16(rows // 2 if n == 2 else 16, LANES),
+                ry=bf16(rows // 2 if n in SPLIT_GROUPS else 16, LANES),
                 q6=sem(4),
             )
             for n, rows in z.rows.items()
@@ -547,9 +559,11 @@
         return SimpleNamespace(mean=mean, inv=inv, gs=scale, sh=bias - mean * scale)
 
     def norm_grad(k, rowu, rowv, width, inv_n, nm):
+        return norm_grad_of(total(k, rowu, width), total(k, rowv, width), width, inv_n, nm)
+
+    def norm_grad_of(su, sv, width, inv_n, nm):
         n = tiled(inv_n, width)
-        su = total(k, rowu, width)
-        sux = nm.inv * (total(k, rowv, width) - nm.mean * su)
+        sux = nm.inv * (sv - nm.mean * su)
         t = sux * n
         return (
             su,
@@ -562,7 +576,7 @@
         def step(i, carry):
             return body(pl.multiple_of(i * tile, tile), carry)
 
-        return lax.fori_loop(0, n // tile, step, init)
+        return lax.fori_loop(0, n // tile, step, init, unroll=2 if n // tile % 2 == 0 else 1)
 
     def zero8(width):
         return jnp.zeros((8, width), F32)
@@ -687,6 +701,57 @@
             )
         return moments(r.blk[k].sp, no, 2 * mid, 32)
 
+    class Meeting:
+        def __init__(self, k):
+            blk = r.blk[k]
+            self.own, self.group, self.ms, self.mr = blk.own, blk.group, blk.ms, blk.mr
+
+        def near(self, to, src):
+            return pltpu.make_async_remote_copy(
+                src_ref=self.own, dst_ref=r.met.at[src], send_sem=self.ms.at[0],
+                recv_sem=self.mr.at[0], device_id=(d, to), device_id_type=MESH,
+            )
+
+        def far(self, to):
+            return pltpu.make_async_remote_copy(
+                src_ref=self.group, dst_ref=r.all.at[d], send_sem=self.ms.at[1],
+                recv_sem=self.mr.at[1], device_id=(to, c), device_id_type=MESH,
+            )
+
+        def wait(self, ref, n):
+            some = ref.at[pl.ds(0, n)]
+            pltpu.make_async_remote_copy(
+                src_ref=some, dst_ref=some, send_sem=self.ms.at[0 if n == nc - 1 else 1],
+                recv_sem=self.mr.at[0 if n == nc - 1 else 1], device_id=partner,
+                device_id_type=MESH,
+            ).wait()
+
+        def start(self):
+            for n in range(1, nc):
+                self.near(chan_at(n), c).start()
+
+        def gather(self):
+            self.wait(r.met, nc - 1)
+            r.met[c] = self.own[...]
+            for kind in range(KINDS):
+                for s in range(nc):
+                    self.group[kind, s * b : (s + 1) * b, :] = r.met[
+                        s, kind * b : (kind + 1) * b, :
+                    ]
+
+        def send(self):
+            def step(j, _):
+                self.far(lax.rem(d + j, nd)).start()
+                return 0
+
+            lax.fori_loop(1, nd, step, 0)
+
+        def finish(self):
+            self.wait(r.all, nd - 1)
+            r.all[d] = self.group[...]
+
+    meet = {k: Meeting(k) for k in (1, 2)}
+
     def attention_forward(k, vr, sync, fills):
         s1, s2 = split_conv(k)
         put(sync, 0, s1)
@@ -695,14 +760,26 @@
         nsplit = norm(sync, 0, 4, 2 * mid, inv_out, v_split(vr.sg), v_split(vr.sb))
         sp, sa, pm = r.blk[k].sp, r.blk[k].sa, r.blk[k].pm
         for img in range(b):
-            def act(at, s, img=img):
+            def act(at, carry, img=img):
+                s, ds, dv = carry
                 rows = pl.ds(pl.multiple_of(at + img * po, 32), 32)
-                v = silu(sp[rows, :] * nsplit.gs + nsplit.sh)
-                v = v * tiled(r.mo[rows, :], 2 * mid)
+                raw = sp[rows, :]
+                v = raw * nsplit.gs + nsplit.sh
+                q = sigmoid(v)
+                qm = q * tiled(r.mo[rows, :], 2 * mid)
+                slope = qm * (1.0 + v * (1.0 - q))
+                v = v * qm
                 sa[rows, :] = v
-                return s + sum8(v)
-
-            s = fold(loop(po, 32, act, zero8(2 * mid)))
+                return s + sum8(v), ds + sum8(slope), dv + sum8(slope * raw)
+
+            zero = zero8(2 * mid)
+            s, ds, dv = (fold(v) for v in loop(po, 32, act, (zero, zero, zero)))
+            own = r.blk[k].own
+            for t in range(4):
+                lanes = slice(t * LANES, (t + 1) * LANES)
+                for kind, v in ((t, ds), (t + 4, dv)):
+                    at = kind * b + img
+                    own[at : at + 1, :] = v[:, lanes] * inv_area[img : img + 1, :]
             pm[img : img + 1, :] = (s[:, :mid] + s[:, mid:]) * tiled(inv_area[img : img + 1, :], mid)
         ex.blk[k].sq.wait()
         squeezed = dot_exact(pm[...], r.blk[k].sq[...])
@@ -717,6 +794,8 @@
         )
         xhat = (squeezed - natt.mean) * natt.inv
         centred = pm[...] - total(sync + 1, 2, mid) * tiled(inv_images, mid)
+        r.blk[k].own[8 * b : 9 * b, :] = xhat[:b, :]
+        meet[k].start()
         pre = squeezed * natt.gs + natt.sh
         excited = silu(pre) * live8
         ex.blk[k].ext.wait()
@@ -770,6 +849,7 @@
         shortcut_forward()
 
     def forward_second():
+        meet[1].gather()
         second_w.wrt.forward()
         for e in (second_w.sq, second_w.ext, second_w.we):
             e.start()
@@ -827,7 +907,8 @@
     lax.fori_loop(0, no // (4 * so), build2, 0)
     im_zero(im2, 0, False)
     im_zero(im2, 2, True)
-    f2 = attention_forward(2, vr2, 5, (None, None, None))
+    f2 = attention_forward(2, vr2, 5, (None, None, meet[2].gather))
+    meet[2].send()
 
     ex.cot.wait()
 
@@ -946,25 +1027,29 @@
             lax.fori_loop(1, n, step, 0)
 
         def total(self, slots, n, to):
+            tile = self.piece if self.piece <= 256 else tile_of(self.piece)
+
             def body(at, _):
-                rows = pl.ds(at, 16)
+                rows = pl.ds(at, tile)
                 t = slots[0, rows, :].astype(F32)
                 for k in range(1, n):
                     t = t + slots[k, rows, :].astype(F32)
                 to[rows, :] = t.astype(BF16)
                 return 0
 
-            loop(self.piece, 16, body, 0)
+            loop(self.piece, tile, body, 0)
 
         def add(self, which, other):
+            tile = tile_of(self.rows)
+
             def body(at, _):
-                rows = pl.ds(at, 128)
+                rows = pl.ds(at, tile)
                 self.pk[which, odd, rows, :] = (
                     self.pk[which, odd, rows, :].astype(F32) + other(rows).astype(F32)
                 ).astype(BF16)
                 return 0
 
-            loop(self.rows, 128, body, 0)
+            loop(self.rows, tile, body, 0)
 
         def step1(self):
             self.copy1().start()
@@ -1077,16 +1162,17 @@
 
         def ready4(self):
             self.copy_half().wait()
+            tile = tile_of(self.half)
 
             def body(at, _):
-                rows = pl.ds(pl.multiple_of(self.par * self.half + at, 16), 16)
+                rows = pl.ds(pl.multiple_of(self.par * self.half + at, 16), tile)
                 self.pk[self.across, odd, rows, :] = (
                     self.pk[self.across, odd, rows, :].astype(F32)
-                    + self.ry[pl.ds(at, 16), :].astype(F32)
+                    + self.ry[pl.ds(at, tile), :].astype(F32)
                 ).astype(BF16)
                 return 0
 
-            loop(self.half, 16, body, 0)
+            loop(self.half, tile, body, 0)
 
         def step4(self):
             self.others(lambda to, _: self.slot3(to, self.far_at).start(), self.far_at, self.quad)
@@ -1133,7 +1219,7 @@
             self.copy_back(self.par).wait_send()
             self.copy_back(1 - self.par).wait_recv()
 
-    sums_of = {group: (SplitReduction if group == 2 else Reduction)(group) for group in GROUPS}
+    sums_of = {group: (SplitReduction if group in SPLIT_GROUPS else Reduction)(group) for group in GROUPS}
 
     def attention_backward(k, f, sync):
         srow = STO_ROWS[k]
@@ -1175,10 +1261,30 @@
         ext = r.blk[k].ext
         excited_grad = dot_exact(l0, ext[0]) + dot_exact(l1, ext[1])
         au = excited_grad * silu_slope(f.pre)
+        sq = r.blk[k].sq
+        sp = r.blk[k].sp
+        r.mgr[...] = dot_exact(natt.gs * au * live8, sq[...], NT) * tiled(inv_area, mid)
+        carry = (zero8(2 * mid), zero8(2 * mid))
+        for img in range(b):
+            def split_up(at, carry, img=img):
+                s1, s2 = carry
+                rows = pl.ds(pl.multiple_of(at + img * po, 32), 32)
+                v = sp[rows, :]
+                slope = tiled(r.mo[rows, :], 2 * mid) * silu_slope(v * nsplit.gs + nsplit.sh)
+                r.su[rows, :] = slope
+                u = slope * (
+                    tiled_pair(r.mg[rows, :]) * at_ref[img : img + 1, :]
+                    + tiled_pair(r.mgr[img : img + 1, :])
+                )
+                return s1 + sum8(u), s2 + sum8(u * v)
+
+            carry = loop(po, 32, split_up, carry)
         put(sync + 1, 0, fold(au))
         put(sync + 1, 1, fold(au * f.xhat))
         put(sync + 1, 2, fold(l0))
         put(sync + 1, 4, fold(l1))
+        put(sync + 1, 6, fold(carry[0]))
+        put(sync + 1, 10, fold(carry[1]))
 
         def matrices():
             r.mixt[...] = jnp.transpose(r.blk[k].mix[...])
@@ -1194,72 +1300,61 @@
                     pack_lanes(k, SHORTCUT, s, dot(r.sgt[...], r.shg[:, share]))
                 sums_of[2].step1()
                 sums_of[5].ready2()
+                sums_of[0].ready4()
                 sums_of[1].ready3()
                 r.pg[...] = dot(r.shg[...], r.wsh[...], NT).astype(BF16)
 
             else:
                 sums_of[0].step1()
 
-        allreduce(sync + 1, 6, matrices)
+        if first:
+            meet[1].finish()
+        allreduce(sync + 1, 14, matrices)
+        if first:
+            sums_of[5].step2()
+            sums_of[2].ready2()
+            sums_of[2].step2()
+            sums_of[0].step4()
+            sums_of[1].step3()
+        else:
+            out_ex[1].start()
         inv_images = 1.0 / (b * nc * nd)
         su, sux = total(sync + 1, 0, att), total(sync + 1, 1, att)
         keep(srow.qb, su)
         keep(srow.qg, sux)
         keep(srow.xb, total(sync + 1, 2, 2 * mid))
-        sb = natt.gs * (au - su * inv_images - f.xhat * (sux * inv_images)) * live8
-        if first:
-            sums_of[1].step3()
-            sums_of[2].ready2()
-            sums_of[2].step2()
-        else:
-            out_ex[1].start()
-        r.mgr[...] = dot_exact(sb, r.blk[k].sq[...], NT) * tiled(inv_area, mid)
-        sp = r.blk[k].sp
-        carry = (zero8(2 * mid), zero8(2 * mid))
+        su, sux = su * inv_images, sux * inv_images
+        sb = natt.gs * (au - su - f.xhat * sux) * live8
+        r.mgr[...] = dot_exact(sb, sq[...], NT) * tiled(inv_area, mid)
+        seen = nd * 8
+        off = dot_exact(natt.gs * (su + r.all[:, 8].reshape(seen, LANES) * sux), sq[...], NT)
+        taken = []
+        for kind in range(8):
+            lanes = slice(kind % 2 * LANES, (kind % 2 + 1) * LANES)
+            taken.append(fold(sum8(off[:, lanes] * r.all[:, kind].reshape(seen, LANES))))
+        su = total(sync + 1, 6, 2 * mid) - jnp.concatenate(taken[:4], axis=1)
+        sv = total(sync + 1, 10, 2 * mid) - jnp.concatenate(taken[4:], axis=1)
+        su, sux, ca, cb = norm_grad_of(su, sv, 2 * mid, inv_out, nsplit)
+        keep(srow.sb, su)
+        keep(srow.sg, sux)
+
+        def split_grad(at, _, img=0):
+            rows = pl.ds(pl.multiple_of(at + img * po, 32), 32)
+            m = tiled(r.mo[rows, :], 2 * mid)
+            u = r.su[rows, :] * (
+                tiled_pair(r.mg[rows, :]) * at_ref[img : img + 1, :]
+                + tiled_pair(r.mgr[img : img + 1, :])
+            )
+            r.sgb[rows, :] = (nsplit.gs * u - m * (ca + cb * sp[rows, :])).astype(BF16)
+            return 0
+
         for img in range(b):
-            def split_up(at, carry, img=img):
-                s1, s2 = carry
-                rows = pl.ds(pl.multiple_of(at + img * po, 32), 32)
-                m = tiled(r.mo[rows, :], 2 * mid)
-                v = sp[rows, :]
-                grad = tiled_pair(r.mg[rows, :]) * at_ref[img : img + 1, :] + tiled_pair(
-                    r.mgr[img : img + 1, :]
-                )
-                u = grad * m * silu_slope(v * nsplit.gs + nsplit.sh)
-                r.su[rows, :] = u
-                return s1 + sum8(u), s2 + sum8(u * v)
-
-            carry = loop(po, 32, split_up, carry)
-        put(sync + 2, 0, fold(carry[0]))
-        put(sync + 2, 4, fold(carry[1]))
+            loop(po, 32, functools.partial(split_grad, img=img), 0)
 
         def squeeze_matrix():
             pack_rows(k, SQUEEZE, 0, dot_exact(f.centred, sb, TN))
-            if first:
-                sums_of[1].ready4()
-            else:
-                sums_of[0].ready2()
-
-        allreduce(sync + 2, 8, squeeze_matrix)
-        if first:
-            sums_of[1].step4()
-            sums_of[5].step2()
-        else:
-            sums_of[0].step2()
-            out_ex[2].start()
-        su, sux, ca, cb = norm_grad(sync + 2, 0, 4, 2 * mid, inv_out, nsplit)
-        keep(srow.sb, su)
-        keep(srow.sg, sux)
-
-        def split_grad(at, _):
-            rows = pl.ds(at, 32)
-            m = tiled(r.mo[rows, :], 2 * mid)
-            r.sgb[rows, :] = (
-                nsplit.gs * r.su[rows, :] - m * (ca + cb * sp[rows, :])
-            ).astype(BF16)
-            return 0
-
-        loop(no, 32, split_grad, 0)
+
+        return squeeze_matrix
 
     def tiled_pair(v):
         return jnp.concatenate([v, v], axis=1)
@@ -1299,7 +1394,8 @@
     def from_right(v):
         return jnp.where(last_g, pltpu.roll(v, tile - 1, 0), 0.0)
 
-    attention_backward(2, f2, 8)
+    meet[2].finish()
+    squeeze_matrix2 = attention_backward(2, f2, 8)
     sums = []
     for g in range(2):
         carry = (zero8(grp), zero8(grp))
@@ -1325,17 +1421,19 @@
 
             carry = loop(po, tile, back2, carry)
         sums.append(carry)
-    put(11, 0, jnp.concatenate([fold(s[0]) for s in sums], axis=1))
-    put(11, 2, jnp.concatenate([fold(s[1]) for s in sums], axis=1))
+    put(10, 0, jnp.concatenate([fold(s[0]) for s in sums], axis=1))
+    put(10, 2, jnp.concatenate([fold(s[1]) for s in sums], axis=1))
     def split_matrix2():
         split_matrix(2)
+        squeeze_matrix2()
         sums_of[1].step1()
-        sums_of[0].ready3()
-
-    allreduce(11, 4, split_matrix2)
-    sums_of[0].step3()
-    out_ex[3].start()
-    su, sux, ca, cb = norm_grad(11, 0, 2, mid, inv_out, nred2)
+        sums_of[0].ready2()
+
+    allreduce(10, 4, split_matrix2)
+    sums_of[0].step2()
+    out_ex[2].start()
+    meet[1].send()
+    su, sux, ca, cb = norm_grad(10, 0, 2, mid, inv_out, nred2)
     keep(STO_ROWS[2].rb, su)
     keep(STO_ROWS[2].rg, sux)
 
@@ -1364,9 +1462,9 @@
         )
 
     s1, s2, s3 = loop(no, 16, first_up, (zero8(co), zero8(co), zero8(co)))
-    put(12, 0, fold(s1))
-    put(12, co // LANES, fold(s2))
-    put(12, 2 * co // LANES, fold(s3))
+    put(11, 0, fold(s1))
+    put(11, co // LANES, fold(s2))
+    put(11, 2 * co // LANES, fold(s3))
 
     def reduce_matrix2():
         r.rgt[:, :no] = jnp.transpose(r.rg1[:no, :])
@@ -1374,13 +1472,17 @@
             pack_rows(2, REDUCE, n0 // LANES, dot(r.rgt[:, :no], r.h[:, n0 : n0 + 256]))
         sums_of[5].step1()
         sums_of[1].ready2()
-        sums_of[0].ready4()
-
-    allreduce(12, 3 * co // LANES, reduce_matrix2)
+        sums_of[0].ready3()
+
+    allreduce(11, 3 * co // LANES, reduce_matrix2)
     sums_of[1].step2()
-    sums_of[0].step4()
-
-    attention_backward(1, f1, 12)
+    sums_of[0].step3()
+    out_ex[3].start()
+
+    squeeze_matrix1 = attention_backward(1, f1, 11)
+    split_matrix(1)
+    squeeze_matrix1()
+    sums_of[3].step1()
     sums = []
     for g in range(2):
         carry = (zero8(grp), zero8(grp))
@@ -1409,20 +1511,19 @@
 
             carry = loop(po, tile, back1, carry)
         sums.append(carry)
-    put(15, 0, jnp.concatenate([fold(s[0]) for s in sums], axis=1))
-    put(15, 2, jnp.concatenate([fold(s[1]) for s in sums], axis=1))
-
-    def split_matrix1():
-        split_matrix(1)
-        sums_of[3].step1()
-        sums_of[2].ready3()
-        sums_of[2].step3()
+    put(13, 0, jnp.concatenate([fold(s[0]) for s in sums], axis=1))
+    put(13, 2, jnp.concatenate([fold(s[1]) for s in sums], axis=1))
+
+    def behind_last():
         sums_of[3].ready2()
+        sums_of[3].step2()
+        sums_of[1].ready4()
         sums_of[5].ready3()
 
-    allreduce(15, 4, split_matrix1)
+    allreduce(13, 4, behind_last)
+    sums_of[1].step4()
     sums_of[5].step3()
-    su, sux, ca, cb = norm_grad(15, 0, 2, mid, inv_in, nred1)
+    su, sux, ca, cb = norm_grad(13, 0, 2, mid, inv_in, nred1)
     keep(STO_ROWS[1].rb, su)
     keep(STO_ROWS[1].rg, sux)
 
@@ -1463,33 +1564,46 @@
     lead = part // (2 * si)
     lax.fori_loop(0, lead, reduce_grad1, 0)
     send_quarter(0)
-    sums_of[3].step2()
-    sums_of[2].ready4()
-    sums_of[2].step4()
+    sums_of[2].ready3()
+    sums_of[2].step3()
     lax.fori_loop(lead, nq * lead, reduce_grad1, 0)
     r.rgt[...] = jnp.transpose(r.rg1[...])
     for n0 in range(0, ci, 256):
         pack_rows(1, REDUCE, n0 // LANES, dot(r.rgt[...], r.x[:, n0 : n0 + 256]))
     sums_of[4].step1()
-    send_quarter(1)
+    sums_of[3].ready3()
+    sums_of[3].step3()
     sums_of[4].ready2()
     sums_of[4].step2()
+    send_quarter(1)
+    sums_of[2].ready4()
+    sums_of[2].step4()
+    sums_of[1].ready5()
+    sums_of[1].step5()
+    sums_of[5].ready4()
+    sums_of[5].step4()
     for q in range(2, nq):
         send_quarter(q)
-    sums_of[5].ready4()
-    sums_of[5].step4()
+    sums_of[3].ready4()
+    sums_of[3].step4()
     sums_of[2].ready5()
     sums_of[2].step5()
-    sums_of[3].ready3()
-    sums_of[3].step3()
+    sums_of[1].ready6()
+    sums_of[1].step6()
+    sums_of[5].ready5()
+    sums_of[5].step5()
     sums_of[4].ready3()
     sums_of[4].step3()
+    sums_of[3].ready5()
+    sums_of[3].step5()
     sums_of[2].ready6()
     sums_of[2].step6()
-    sums_of[3].ready4()
-    sums_of[3].step4()
+    sums_of[5].ready6()
+    sums_of[5].step6()
     sums_of[4].ready4()
     sums_of[4].step4()
+    sums_of[3].ready6()
+    sums_of[3].step6()
     for e in out_ex + last:
         e.wait()
     for sums in sums_of.values():

time: 229 us -> 226 us (0.987)
  Pallas kernels: 228 us -> 225 us
    pallas_call x1, Pallas kernels: 221 us -> 218 us  [per_device(): pl.pallas_call(functools.partial(mega_kernel, z, tree), out_shape=jax.tre...]
where the time goes in v3:
time: 226 us
  Pallas kernels  225 us (100%)
    pallas_call x1, Pallas kernels, per_device(): pl.pallas_call(functools.partial(mega_kernel, z, tree), out_shape=jax.tre...  218 us
    pallas_call x1, Pallas kernels, unpack(): pl.pallas_call(functools.partial(unpack_kernel, z, plan, jax.tree.structu...  6.71 us

profile of v3, /device:TPU:0, one launch (start us, length us, event | category | flops | bytes accessed | tf_op | source)
XLA Modules:
  0.0 225.9 jit_solution(10184455708388885296)
XLA Ops:
  0.7 218.3 %two_blocks.1 = (bf16[8192,128]{1,0:T(8,128)(2,1)}, bf16[2048,256]{1,0:T(8,128)(2,1)}, bf16[640,128]{1,0:T(8,128)(2,1)}, bf16[1280,128]{1,0:T(8,128)(2,1)}, bf16...) custom-call(bf16[2,64,128]{2,1,0:T(8,128)(2,1)} %bitcast.62, ...), custom_call_target="tpu_custom_call" | custom-call | tf_op jit(solution)/shard_map/two_blocks/pallas_call | solution.py:1667
  219.0 6.7 %unpack.1 = (f32[2048,256]{1,0:T(8,128)}, f32[8192,128]{1,0:T(8,128)}, f32[64,512]{1,0:T(8,128)}, f32[1,64]{1,0:T(1,128)}, f32[1,64]{1,0:T(1,128)}, /*index=5*/f...) custom-call(bf16[8192,128]{1,0:T(8,128)(2,1)} %get-tuple-element.75., ...), custom_call_target="tpu_custom_call" | custom-call | tf_op jit(solution)/shard_map/unpack/pallas_call | solution.py:1753

commit v4 on v3

--- a/solution.py
+++ b/solution.py
@@ -120,7 +120,7 @@
     4: ((1, REDUCE),),
     5: ((2, REDUCE),),
 }
-SPLIT_GROUPS = (1, 2, 3, 5)
+SPLIT_GROUPS = (1, 2, 3)
 VEC_ROWS = {
     1: SimpleNamespace(rg=0, rb=1, sg=2, sb=4, xb=6, eg=8, eb=10, hg=12, hb=14, qg=16, qb=17),
     2: SimpleNamespace(rg=18, rb=19, sg=20, sb=22, xb=24, eg=26, eb=28, qg=30, qb=31),
@@ -1318,6 +1318,7 @@
             sums_of[1].step3()
         else:
             out_ex[1].start()
+            out_ex[2].start()
         inv_images = 1.0 / (b * nc * nd)
         su, sux = total(sync + 1, 0, att), total(sync + 1, 1, att)
         keep(srow.qb, su)
@@ -1431,7 +1432,7 @@
 
     allreduce(10, 4, split_matrix2)
     sums_of[0].step2()
-    out_ex[2].start()
+    out_ex[3].start()
     meet[1].send()
     su, sux, ca, cb = norm_grad(10, 0, 2, mid, inv_out, nred2)
     keep(STO_ROWS[2].rb, su)
@@ -1477,7 +1478,6 @@
     allreduce(11, 3 * co // LANES, reduce_matrix2)
     sums_of[1].step2()
     sums_of[0].step3()
-    out_ex[3].start()
 
     squeeze_matrix1 = attention_backward(1, f1, 11)
     split_matrix(1)
@@ -1518,11 +1518,9 @@
         sums_of[3].ready2()
         sums_of[3].step2()
         sums_of[1].ready4()
-        sums_of[5].ready3()
 
     allreduce(13, 4, behind_last)
     sums_of[1].step4()
-    sums_of[5].step3()
     su, sux, ca, cb = norm_grad(13, 0, 2, mid, inv_in, nred1)
     keep(STO_ROWS[1].rb, su)
     keep(STO_ROWS[1].rg, sux)
@@ -1564,6 +1562,8 @@
     lead = part // (2 * si)
     lax.fori_loop(0, lead, reduce_grad1, 0)
     send_quarter(0)
+    sums_of[5].ready3()
+    sums_of[5].step3()
     sums_of[2].ready3()
     sums_of[2].step3()
     lax.fori_loop(lead, nq * lead, reduce_grad1, 0)
@@ -1580,26 +1580,22 @@
     sums_of[2].step4()
     sums_of[1].ready5()
     sums_of[1].step5()
+    for q in range(2, nq):
+        send_quarter(q)
     sums_of[5].ready4()
     sums_of[5].step4()
-    for q in range(2, nq):
-        send_quarter(q)
     sums_of[3].ready4()
     sums_of[3].step4()
     sums_of[2].ready5()
     sums_of[2].step5()
     sums_of[1].ready6()
     sums_of[1].step6()
-    sums_of[5].ready5()
-    sums_of[5].step5()
     sums_of[4].ready3()
     sums_of[4].step3()
     sums_of[3].ready5()
     sums_of[3].step5()
     sums_of[2].ready6()
     sums_of[2].step6()
-    sums_of[5].ready6()
-    sums_of[5].step6()
     sums_of[4].ready4()
     sums_of[4].step4()
     sums_of[3].ready6()

time: 226 us -> 223 us (0.987)
  Pallas kernels: 225 us -> 222 us
    pallas_call x1, Pallas kernels: 218 us -> 216 us  [per_device(): pl.pallas_call(functools.partial(mega_kernel, z, tree), out_shape=jax.tre...]
where the time goes in v4:
time: 223 us
  Pallas kernels  222 us (100%)
    pallas_call x1, Pallas kernels, per_device(): pl.pallas_call(functools.partial(mega_kernel, z, tree), out_shape=jax.tre...  216 us
    pallas_call x1, Pallas kernels, unpack(): pl.pallas_call(functools.partial(unpack_kernel, z, plan, jax.tree.structu...  6.71 us

profile of v4, /device:TPU:0, one launch (start us, length us, event | category | flops | bytes accessed | tf_op | source)
XLA Modules:
  0.0 223.1 jit_solution(4168452343249872422)
XLA Ops:
  0.7 215.5 %two_blocks.1 = (bf16[8192,128]{1,0:T(8,128)(2,1)}, bf16[2048,256]{1,0:T(8,128)(2,1)}, bf16[640,128]{1,0:T(8,128)(2,1)}, bf16[1280,128]{1,0:T(8,128)(2,1)}, bf16...) custom-call(bf16[2,64,128]{2,1,0:T(8,128)(2,1)} %bitcast.62, ...), custom_call_target="tpu_custom_call" | custom-call | tf_op jit(solution)/shard_map/two_blocks/pallas_call | solution.py:1663
  216.2 6.7 %unpack.1 = (f32[2048,256]{1,0:T(8,128)}, f32[8192,128]{1,0:T(8,128)}, f32[64,512]{1,0:T(8,128)}, f32[1,64]{1,0:T(1,128)}, f32[1,64]{1,0:T(1,128)}, /*index=5*/f...) custom-call(bf16[8192,128]{1,0:T(8,128)(2,1)} %get-tuple-element.75., ...), custom_call_target="tpu_custom_call" | custom-call | tf_op jit(solution)/shard_map/unpack/pallas_call | solution.py:1749
